TPU v7x, 32 devices: a whole 2x2x4 slice. The times are simulated.
32 devices in a mesh: rep: 8 (over z, y), shard: 4 (over x, core).
Axes of the slice: x: 2, y: 2, z: 4, core: 2. Of those that a mesh axis runs over, the one named last changes fastest.
Arguments:
- tokens: bfloat16 [16, 1024, 1536], P('rep', 'shard'), may hold values from -6 to 6
- cotangent: bfloat16 [16, 1024, 1536], P('rep', 'shard'), may hold values from -6 to 6
- prefix_len: int32 [16], P('rep'), may hold values from 102 to 512
- adapter_index: int32 [16], P('rep'), may hold values from 0 to 7
- gain_attn: bfloat16 [1536], replicated, may hold values from 0.099609375 to 1.8984375
- gain_mlp: bfloat16 [1536], replicated, may hold values from 0.099609375 to 1.8984375
- query_weight: bfloat16 [1536, 1536], P('shard'), may hold values from -0.15625 to 0.15625
- key_weight: bfloat16 [1536, 768], P('shard'), may hold values from -0.15625 to 0.15625
- value_weight: bfloat16 [1536, 768], P('shard'), may hold values from -0.15625 to 0.15625
- output_weight: bfloat16 [1536, 1536], P('shard'), may hold values from -2.5 to 2.5
- gate_weight: bfloat16 [1536, 4096], P('shard'), may hold values from -0.15625 to 0.15625
- lift_weight: bfloat16 [1536, 4096], P('shard'), may hold values from -0.15625 to 0.15625
- drop_weight: bfloat16 [4096, 1536], P('shard'), may hold values from -0.09375 to 0.09375
- query_inner: bfloat16 [1536, 128], P('shard'), may hold values from -0.15625 to 0.15625
- query_outer: bfloat16 [128, 1536], P(None, 'shard'), may hold values from -0.75 to 0.75
- key_inner: bfloat16 [1536, 128], P('shard'), may hold values from -0.15625 to 0.15625
- key_outer: bfloat16 [128, 768], P(None, 'shard'), may hold values from -0.75 to 0.75
- value_inner: bfloat16 [1536, 128], P('shard'), may hold values from -0.15625 to 0.15625
- value_outer: bfloat16 [128, 768], P(None, 'shard'), may hold values from -0.75 to 0.75
- output_inner: bfloat16 [1536, 128], P('shard'), may hold values from -2.5 to 2.5
- output_outer: bfloat16 [128, 1536], P(None, 'shard'), may hold values from -0.75 to 0.75
- gate_inner: bfloat16 [1536, 128], P('shard'), may hold values from -0.15625 to 0.15625
- gate_outer: bfloat16 [128, 4096], P(None, 'shard'), may hold values from -0.75 to 0.75
- lift_inner: bfloat16 [1536, 128], P('shard'), may hold values from -0.15625 to 0.15625
- lift_outer: bfloat16 [128, 4096], P(None, 'shard'), may hold values from -0.75 to 0.75
- drop_inner: bfloat16 [4096, 128], P('shard'), may hold values from -0.09375 to 0.09375
- drop_outer: bfloat16 [128, 1536], P(None, 'shard'), may hold values from -0.75 to 0.75
Outputs:
- mixed: bfloat16 [16, 1024, 1536], P('rep', 'shard')
- input_grad: float32 [16, 1024, 1536], P('rep', 'shard')
- query_inner_grad: float32 [1536, 128], P('shard')
- query_outer_grad: float32 [128, 1536], P(None, 'shard')
- key_inner_grad: float32 [1536, 128], P('shard')
- key_outer_grad: float32 [128, 768], P(None, 'shard')
- value_inner_grad: float32 [1536, 128], P('shard')
- value_outer_grad: float32 [128, 768], P(None, 'shard')
- output_inner_grad: float32 [1536, 128], P('shard')
- output_outer_grad: float32 [128, 1536], P(None, 'shard')
- gate_inner_grad: float32 [1536, 128], P('shard')
- gate_outer_grad: float32 [128, 4096], P(None, 'shard')
- lift_inner_grad: float32 [1536, 128], P('shard')
- lift_outer_grad: float32 [128, 4096], P(None, 'shard')
- drop_inner_grad: float32 [4096, 128], P('shard')
- drop_outer_grad: float32 [128, 1536], P(None, 'shard')
All inputs are finite; a program needn't handle non-finite values.
Results may differ from a plain program's by a relative error of at most 0.02.
Values may be sent and summed in bfloat16 or wider, within the bound.
No kernel may reach another device: no remote copies, remote signals or barrier semaphores. Data moves between devices by JAX's collectives and lax.ppermute only.
A program may use at most 208 MiB of HBM per device.

v0:
```python
import math

import jax
import jax.numpy as jnp
from jax import lax
from jax.sharding import PartitionSpec as P

HEADS = 16
KV_HEADS = 8
HEAD_DIM = 96
RANK = 16
ADAPTERS = 8


EPSILON = 1e-05
ROPE_BASE = 100000.0
MASKED_SCORE = -1e30


def rotary_tables(positions, head_dim):
    half_dim = head_dim // 2
    freq_index = jnp.arange(half_dim).astype(jnp.float32)
    frequency = jnp.exp(freq_index * (-2.0 * math.log(ROPE_BASE) / head_dim))
    angles = positions[:, None] * frequency[None, :]
    return (jnp.cos(angles)[:, None, :], jnp.sin(angles)[:, None, :])


def rotate(inputs, cos_table, sine_table):
    half_dim = inputs.shape[-1] // 2
    first_half = inputs[..., :half_dim]
    second_half = inputs[..., half_dim:]
    return jnp.concatenate(
        [
            first_half * cos_table - second_half * sine_table,
            second_half * cos_table + first_half * sine_table,
        ],
        axis=-1,
    )


def rotate_back(out_grad, cos_table, sine_table):
    half_dim = out_grad.shape[-1] // 2
    first_half = out_grad[..., :half_dim]
    second_half = out_grad[..., half_dim:]
    return jnp.concatenate(
        [
            first_half * cos_table + second_half * sine_table,
            second_half * cos_table - first_half * sine_table,
        ],
        axis=-1,
    )


def rms_scale(inputs):
    return lax.rsqrt(jnp.mean(inputs * inputs, axis=-1, keepdims=True) + EPSILON)


def norm_back(out_grad, normed, scale_rows, gain):
    scaled = out_grad * gain
    return scale_rows * (scaled - normed * jnp.mean(scaled * normed, axis=-1, keepdims=True))


def project(source, weight, inner_mat, outer_mat, onehot):
    hidden = (jnp.dot(source, inner_mat, preferred_element_type=jnp.float32) * onehot).astype(
        jnp.bfloat16
    )
    result = jnp.dot(source, weight, preferred_element_type=jnp.float32) + jnp.dot(
        hidden, outer_mat, preferred_element_type=jnp.float32
    )
    return (result, hidden)


def project_back(out_grad, weight, inner_mat, outer_mat, onehot):
    hidden_grad = (
        jnp.einsum("to,mo->tm", out_grad, outer_mat, preferred_element_type=jnp.float32) * onehot
    ).astype(jnp.bfloat16)
    source_grad = jnp.einsum(
        "to,io->ti", out_grad, weight, preferred_element_type=jnp.float32
    ) + jnp.einsum("tm,im->ti", hidden_grad, inner_mat, preferred_element_type=jnp.float32)
    return (source_grad, hidden_grad)


def full_pair(out_grad, source, hidden, hidden_grad):
    inner_grad = jnp.einsum("ti,tm->im", source, hidden_grad, preferred_element_type=jnp.float32)
    outer_grad = jnp.einsum("tm,to->mo", hidden, out_grad, preferred_element_type=jnp.float32)
    return (inner_grad, outer_grad)


def masked_scores(query_five, all_keys, allowed, score_scale):
    raw_scores = (
        jnp.einsum("sqkgd,sjkd->skgqj", query_five, all_keys, preferred_element_type=jnp.float32)
        * score_scale
    )
    return jnp.where(allowed[:, None, None], raw_scores, MASKED_SCORE)


def attend(query_five, all_keys, all_values, allowed, score_scale):
    scores = masked_scores(query_five, all_keys, allowed, score_scale)
    top_score = jnp.max(scores, axis=-1, keepdims=True)
    expo = jnp.exp(scores - top_score)
    total = jnp.sum(expo, axis=-1, keepdims=True)
    probs_low = (expo / total).astype(jnp.bfloat16)
    log_total = top_score + jnp.log(total)
    attended = jnp.einsum(
        "skgqj,sjkd->sqkgd", probs_low, all_values, preferred_element_type=jnp.float32
    )
    return (attended, log_total)


def attend_back(query_five, all_keys, all_values, allowed, log_total, grad_five, score_scale):
    scores_again = masked_scores(query_five, all_keys, allowed, score_scale)
    probs_full = jnp.exp(scores_again - log_total)
    probs_again = probs_full.astype(jnp.bfloat16)
    value_full_grad = jnp.einsum(
        "skgqj,sqkgd->sjkd", probs_again, grad_five, preferred_element_type=jnp.float32
    )
    probs_grad = jnp.einsum(
        "sqkgd,sjkd->skgqj", grad_five, all_values, preferred_element_type=jnp.float32
    )
    score_grad = (
        probs_full * (probs_grad - jnp.sum(probs_full * probs_grad, axis=-1, keepdims=True))
    ).astype(jnp.bfloat16)
    query_rot_grad = (
        jnp.einsum("skgqj,sjkd->sqkgd", score_grad, all_keys, preferred_element_type=jnp.float32)
        * score_scale
    )
    key_full_grad = (
        jnp.einsum("skgqj,sqkgd->sjkd", score_grad, query_five, preferred_element_type=jnp.float32)
        * score_scale
    )
    return (query_rot_grad, key_full_grad, value_full_grad)


def local(
    tokens,
    cotangent,
    prefix_len,
    adapter_index,
    gain_attn,
    gain_mlp,
    query_weight,
    key_weight,
    value_weight,
    output_weight,
    gate_weight,
    lift_weight,
    drop_weight,
    query_inner,
    query_outer,
    key_inner,
    key_outer,
    value_inner,
    value_outer,
    output_inner,
    output_outer,
    gate_inner,
    gate_outer,
    lift_inner,
    lift_outer,
    drop_inner,
    drop_outer,
):
    sequences, local_len, model_width = tokens.shape
    shard_count = lax.axis_size("shard")
    full_len = local_len * shard_count
    group_size = HEADS // KV_HEADS
    kv_width = KV_HEADS * HEAD_DIM
    tok_rows = sequences * local_len
    score_scale = HEAD_DIM ** (-0.5)
    f32 = jnp.float32
    bf16 = jnp.bfloat16
    column_owner = jnp.arange(ADAPTERS * RANK) // RANK
    seq_onehot = (column_owner[None, :] == adapter_index[:, None]).astype(f32)
    onehot = jnp.broadcast_to(
        seq_onehot[:, None, :], (sequences, local_len, ADAPTERS * RANK)
    ).reshape(tok_rows, ADAPTERS * RANK)

    def pair_grads(out_grad, source, hidden, hidden_grad):
        return full_pair(out_grad, source, hidden, hidden_grad)

    attn_full = (
        lax.all_gather(query_weight, "shard", axis=0, tiled=True),
        lax.all_gather(key_weight, "shard", axis=0, tiled=True),
        lax.all_gather(value_weight, "shard", axis=0, tiled=True),
        lax.all_gather(output_weight, "shard", axis=0, tiled=True),
        lax.all_gather(query_inner, "shard", axis=0, tiled=True),
        lax.all_gather(query_outer, "shard", axis=1, tiled=True),
        lax.all_gather(key_inner, "shard", axis=0, tiled=True),
        lax.all_gather(key_outer, "shard", axis=1, tiled=True),
        lax.all_gather(value_inner, "shard", axis=0, tiled=True),
        lax.all_gather(value_outer, "shard", axis=1, tiled=True),
        lax.all_gather(output_inner, "shard", axis=0, tiled=True),
        lax.all_gather(output_outer, "shard", axis=1, tiled=True),
    )
    inputs = tokens.reshape(tok_rows, model_width).astype(f32)
    gain_one = gain_attn.astype(f32)
    gain_two = gain_mlp.astype(f32)
    scale_one = rms_scale(inputs)
    normed_one = inputs * scale_one
    normed_attn = (normed_one * gain_one).astype(bf16)
    query_pre, query_hidden = project(normed_attn, attn_full[0], attn_full[4], attn_full[5], onehot)
    key_pre, key_hidden = project(normed_attn, attn_full[1], attn_full[6], attn_full[7], onehot)
    value_pre, value_hidden = project(normed_attn, attn_full[2], attn_full[8], attn_full[9], onehot)
    query_pos = lax.axis_index("shard") * local_len + jnp.arange(local_len)
    cos_table, sine_table = rotary_tables(query_pos.astype(f32), HEAD_DIM)
    query_rot = rotate(
        query_pre.reshape(sequences, local_len, HEADS, HEAD_DIM), cos_table, sine_table
    ).astype(bf16)
    key_rot = rotate(
        key_pre.reshape(sequences, local_len, KV_HEADS, HEAD_DIM), cos_table, sine_table
    ).astype(bf16)
    value_low = value_pre.reshape(sequences, local_len, KV_HEADS, HEAD_DIM).astype(bf16)
    key_pos = jnp.arange(full_len)
    all_keys, all_values = (
        lax.all_gather(key_rot, "shard", axis=1, tiled=True),
        lax.all_gather(value_low, "shard", axis=1, tiled=True),
    )
    allowed = (key_pos[None, None, :] <= query_pos[None, :, None]) | (
        key_pos[None, None, :] < prefix_len[:, None, None]
    )
    query_five = query_rot.reshape(sequences, local_len, KV_HEADS, group_size, HEAD_DIM)
    pos_attended, log_total = attend(query_five, all_keys, all_values, allowed, score_scale)
    attended = pos_attended.reshape(tok_rows, model_width).astype(bf16)
    mlp_full = (
        lax.all_gather(gate_weight, "shard", axis=0, tiled=True),
        lax.all_gather(lift_weight, "shard", axis=0, tiled=True),
        lax.all_gather(drop_weight, "shard", axis=0, tiled=True),
        lax.all_gather(gate_inner, "shard", axis=0, tiled=True),
        lax.all_gather(gate_outer, "shard", axis=1, tiled=True),
        lax.all_gather(lift_inner, "shard", axis=0, tiled=True),
        lax.all_gather(lift_outer, "shard", axis=1, tiled=True),
        lax.all_gather(drop_inner, "shard", axis=0, tiled=True),
        lax.all_gather(drop_outer, "shard", axis=1, tiled=True),
    )
    branch_out, output_hidden = project(
        attended, attn_full[3], attn_full[10], attn_full[11], onehot
    )
    middle = inputs + branch_out
    scale_two = rms_scale(middle)
    normed_two = middle * scale_two
    normed_mlp = (normed_two * gain_two).astype(bf16)
    gate_act, gate_hidden = project(normed_mlp, mlp_full[0], mlp_full[3], mlp_full[4], onehot)
    lift_act, lift_hidden = project(normed_mlp, mlp_full[1], mlp_full[5], mlp_full[6], onehot)
    sigmoid_gate = jax.nn.sigmoid(gate_act)
    silu_gate = gate_act * sigmoid_gate
    active = (silu_gate * lift_act).astype(bf16)
    drop_out, drop_hidden = project(active, mlp_full[2], mlp_full[7], mlp_full[8], onehot)
    mixed = (middle + drop_out).astype(bf16).reshape(sequences, local_len, model_width)
    mlp_back = (
        lax.all_gather(gate_weight, "shard", axis=0, tiled=True),
        lax.all_gather(lift_weight, "shard", axis=0, tiled=True),
        lax.all_gather(drop_weight, "shard", axis=0, tiled=True),
        lax.all_gather(gate_inner, "shard", axis=0, tiled=True),
        lax.all_gather(gate_outer, "shard", axis=1, tiled=True),
        lax.all_gather(lift_inner, "shard", axis=0, tiled=True),
        lax.all_gather(lift_outer, "shard", axis=1, tiled=True),
        lax.all_gather(drop_inner, "shard", axis=0, tiled=True),
        lax.all_gather(drop_outer, "shard", axis=1, tiled=True),
    )
    cot_rows = cotangent.reshape(tok_rows, model_width)
    active_grad, drop_hgrad = project_back(cot_rows, mlp_back[2], mlp_back[7], mlp_back[8], onehot)
    drop_inner_grad, drop_outer_grad = pair_grads(cot_rows, active, drop_hidden, drop_hgrad)
    gate_grad = (
        active_grad * lift_act * sigmoid_gate * (1.0 + gate_act * (1.0 - sigmoid_gate))
    ).astype(bf16)
    lift_grad = (active_grad * silu_gate).astype(bf16)
    mlp_in_gate, gate_hgrad = project_back(gate_grad, mlp_back[0], mlp_back[3], mlp_back[4], onehot)
    gate_inner_grad, gate_outer_grad = pair_grads(gate_grad, normed_mlp, gate_hidden, gate_hgrad)
    mlp_in_lift, lift_hgrad = project_back(lift_grad, mlp_back[1], mlp_back[5], mlp_back[6], onehot)
    lift_inner_grad, lift_outer_grad = pair_grads(lift_grad, normed_mlp, lift_hidden, lift_hgrad)
    middle_grad = cot_rows.astype(f32) + norm_back(
        mlp_in_gate + mlp_in_lift, normed_two, scale_two, gain_two
    )
    attn_back = (
        lax.all_gather(query_weight, "shard", axis=0, tiled=True),
        lax.all_gather(key_weight, "shard", axis=0, tiled=True),
        lax.all_gather(value_weight, "shard", axis=0, tiled=True),
        lax.all_gather(output_weight, "shard", axis=0, tiled=True),
        lax.all_gather(query_inner, "shard", axis=0, tiled=True),
        lax.all_gather(query_outer, "shard", axis=1, tiled=True),
        lax.all_gather(key_inner, "shard", axis=0, tiled=True),
        lax.all_gather(key_outer, "shard", axis=1, tiled=True),
        lax.all_gather(value_inner, "shard", axis=0, tiled=True),
        lax.all_gather(value_outer, "shard", axis=1, tiled=True),
        lax.all_gather(output_inner, "shard", axis=0, tiled=True),
        lax.all_gather(output_outer, "shard", axis=1, tiled=True),
    )
    branch_grad = middle_grad.astype(bf16)
    attended_grad, output_hgrad = project_back(
        branch_grad, attn_back[3], attn_back[10], attn_back[11], onehot
    )
    output_inner_grad, output_outer_grad = pair_grads(
        branch_grad, attended, output_hidden, output_hgrad
    )
    attended_low = attended_grad.astype(bf16)
    grad_five = attended_low.reshape(sequences, local_len, KV_HEADS, group_size, HEAD_DIM)
    query_rot_grad, key_full_grad, value_full_grad = attend_back(
        query_five, all_keys, all_values, allowed, log_total, grad_five, score_scale
    )
    key_local_grad, value_local_grad = (
        lax.psum_scatter(
            key_full_grad.astype(jnp.bfloat16), "shard", scatter_dimension=1, tiled=True
        ).astype(jnp.float32),
        lax.psum_scatter(
            value_full_grad.astype(jnp.bfloat16), "shard", scatter_dimension=1, tiled=True
        ).astype(jnp.float32),
    )
    query_grad = (
        rotate_back(
            query_rot_grad.reshape(sequences, local_len, HEADS, HEAD_DIM), cos_table, sine_table
        )
        .reshape(tok_rows, model_width)
        .astype(bf16)
    )
    key_grad = (
        rotate_back(key_local_grad, cos_table, sine_table).reshape(tok_rows, kv_width).astype(bf16)
    )
    value_grad = value_local_grad.reshape(tok_rows, kv_width).astype(bf16)
    attn_in_query, query_hgrad = project_back(
        query_grad, attn_back[0], attn_back[4], attn_back[5], onehot
    )
    query_inner_grad, query_outer_grad = pair_grads(
        query_grad, normed_attn, query_hidden, query_hgrad
    )
    attn_in_key, key_hgrad = project_back(
        key_grad, attn_back[1], attn_back[6], attn_back[7], onehot
    )
    key_inner_grad, key_outer_grad = pair_grads(key_grad, normed_attn, key_hidden, key_hgrad)
    attn_in_value, value_hgrad = project_back(
        value_grad, attn_back[2], attn_back[8], attn_back[9], onehot
    )
    value_inner_grad, value_outer_grad = pair_grads(
        value_grad, normed_attn, value_hidden, value_hgrad
    )
    input_grad = middle_grad + norm_back(
        attn_in_query + attn_in_key + attn_in_value, normed_one, scale_one, gain_one
    )
    input_grad = input_grad.reshape(sequences, local_len, model_width)
    grads = (
        query_inner_grad,
        query_outer_grad,
        key_inner_grad,
        key_outer_grad,
        value_inner_grad,
        value_outer_grad,
        output_inner_grad,
        output_outer_grad,
        gate_inner_grad,
        gate_outer_grad,
        lift_inner_grad,
        lift_outer_grad,
        drop_inner_grad,
        drop_outer_grad,
    )
    owned = (
        lax.psum_scatter(
            grads[0].astype(jnp.bfloat16), "shard", scatter_dimension=0, tiled=True
        ).astype(jnp.float32),
        lax.psum_scatter(
            grads[1].astype(jnp.bfloat16), "shard", scatter_dimension=1, tiled=True
        ).astype(jnp.float32),
        lax.psum_scatter(
            grads[2].astype(jnp.bfloat16), "shard", scatter_dimension=0, tiled=True
        ).astype(jnp.float32),
        lax.psum_scatter(
            grads[3].astype(jnp.bfloat16), "shard", scatter_dimension=1, tiled=True
        ).astype(jnp.float32),
        lax.psum_scatter(
            grads[4].astype(jnp.bfloat16), "shard", scatter_dimension=0, tiled=True
        ).astype(jnp.float32),
        lax.psum_scatter(
            grads[5].astype(jnp.bfloat16), "shard", scatter_dimension=1, tiled=True
        ).astype(jnp.float32),
        lax.psum_scatter(
            grads[6].astype(jnp.bfloat16), "shard", scatter_dimension=0, tiled=True
        ).astype(jnp.float32),
        lax.psum_scatter(
            grads[7].astype(jnp.bfloat16), "shard", scatter_dimension=1, tiled=True
        ).astype(jnp.float32),
        lax.psum_scatter(
            grads[8].astype(jnp.bfloat16), "shard", scatter_dimension=0, tiled=True
        ).astype(jnp.float32),
        lax.psum_scatter(
            grads[9].astype(jnp.bfloat16), "shard", scatter_dimension=1, tiled=True
        ).astype(jnp.float32),
        lax.psum_scatter(
            grads[10].astype(jnp.bfloat16), "shard", scatter_dimension=0, tiled=True
        ).astype(jnp.float32),
        lax.psum_scatter(
            grads[11].astype(jnp.bfloat16), "shard", scatter_dimension=1, tiled=True
        ).astype(jnp.float32),
        lax.psum_scatter(
            grads[12].astype(jnp.bfloat16), "shard", scatter_dimension=0, tiled=True
        ).astype(jnp.float32),
        lax.psum_scatter(
            grads[13].astype(jnp.bfloat16), "shard", scatter_dimension=1, tiled=True
        ).astype(jnp.float32),
    )
    summed = lax.psum(
        (
            owned[0],
            owned[1],
            owned[2],
            owned[3],
            owned[4],
            owned[5],
            owned[6],
            owned[7],
            owned[8],
            owned[9],
            owned[10],
            owned[11],
            owned[12],
            owned[13],
        ),
        "rep",
    )
    return (
        mixed,
        input_grad,
        summed[0],
        summed[1],
        summed[2],
        summed[3],
        summed[4],
        summed[5],
        summed[6],
        summed[7],
        summed[8],
        summed[9],
        summed[10],
        summed[11],
        summed[12],
        summed[13],
    )


def solution(mesh):
    placed = (
        P("rep", "shard", None),
        P("rep", "shard", None),
        P("rep"),
        P("rep"),
        P(),
        P(),
        P("shard", None),
        P("shard", None),
        P("shard", None),
        P("shard", None),
        P("shard", None),
        P("shard", None),
        P("shard", None),
        P("shard", None),
        P(None, "shard"),
        P("shard", None),
        P(None, "shard"),
        P("shard", None),
        P(None, "shard"),
        P("shard", None),
        P(None, "shard"),
        P("shard", None),
        P(None, "shard"),
        P("shard", None),
        P(None, "shard"),
        P("shard", None),
        P(None, "shard"),
    )
    return jax.shard_map(
        local,
        mesh=mesh,
        in_specs=placed,
        out_specs=(
            P("rep", "shard", None),
            P("rep", "shard", None),
            P("shard", None),
            P(None, "shard"),
            P("shard", None),
            P(None, "shard"),
            P("shard", None),
            P(None, "shard"),
            P("shard", None),
            P(None, "shard"),
            P("shard", None),
            P(None, "shard"),
            P("shard", None),
            P(None, "shard"),
            P("shard", None),
            P(None, "shard"),
        ),
        check_vma=False,
    )
```

profile of v0, /device:TPU:0, one launch (start us, length us, event | category | flops | bytes accessed | tf_op | source)
XLA Modules:
  0.0 1198.2 jit_solution(3976422786376973747)
XLA Ops:
  10.0 7.9 all_gather.95
  19.9 6.8 all_gather.96
  27.0 10.5 all-gather.17.cloned.1.call-done
  53.8 9.0 all_gather.91
  81.1 9.2 all_gather.99
  90.3 9.5 all_gather.100
  99.8 9.5 all_gather.102
  109.3 6.8 all_gather.103
  116.1 7.0 all_gather.105
  123.1 9.5 all_gather.108
  132.6 9.0 all_gather.112
  160.3 15.9 %fusion.62 = (f32[2,8,2,256]{3,2,1,0:T(2,128)S(1)}, f32[2,8,2,256,1024]{3,4,2,1,0:T(8,128)}) fusion(bf16[2,256,8,2,48]{1,4,3,2,0:T(8,128)(2,1)S(1)} %bitcast.280, bf16[2,256,8,2,48]{1,4,3,2,0:T(8,128)(2,1)S(1)} %bitcast.278, bf16[2,1024,8,96]{1,3,2,0:T(8,128)(2,1)} %all-gather.19.cloned.1.call-done, pred[2,256,1024]{1,2,0:T(8,128)(4,1)S(1)} %copy-done.19), kind=kOutput, calls=%fused_computation.145 | convolution fusion | flops 1638916096 | bytes 38830080 | tf_op jit(solution)/shard_map/sqkgd,sjkd->skgqj/dot_general | solution.py:91
  176.3 13.9 %fusion.3 = f32[2,8,2,256]{3,2,1,0:T(2,128)S(1)} fusion(f32[2,8,2,256,1024]{3,4,2,1,0:T(8,128)} %get-tuple-element.48, f32[2,8,2,256]{3,2,1,0:T(2,128)S(1)} %get-tuple-element.47), kind=kLoop, calls=%fused_computation.9 | loop fusion | flops 16769024 | bytes 33619968 | tf_op jit(solution)/shard_map/reduce_sum | solution.py:101
  190.8 15.0 %fusion.36 = bf16[2,256,8,2,96]{1,4,3,2,0:T(8,128)(2,1)S(1)} fusion(f32[2,8,2,256,1024]{3,4,2,1,0:T(8,128)} %get-tuple-element.48, f32[2,8,2,256]{3,2,1,0:T(2,128)S(1)} %fusion.3, f32[2,8,2,256]{3,2,1,0:T(2,128)S(1)} %get-tuple-element.47, bf16[2,1024,8,96]{1,3,2,0:T(8,128)(2,1)} %all-gather.15.cloned.1.call-done), kind=kOutput, calls=%fused_computation.96 | convolution fusion | flops 1636564992 | bytes 38338560 | tf_op jit(solution)/shard_map/skgqj,sjkd->sqkgd/dot_general | solution.py:104
  209.1 6.0 all-gather.23.cloned.1.call-done
  224.7 74.0 %all-gather.33.cloned.1.call-done = bf16[4096,1536]{1,0:T(8,128)(2,1)} async-done(((bf16[1024,1536]{1,0:T(8,128)(2,1)}), bf16[4096,1536]{1,0:T(8,128)(2,1)}) %all-gather.33.cloned.1.call-update) | async-done | bytes 12582928 | tf_op jit(solution)/shard_map/all_gather | solution.py:227
  298.8 12.4 %fusion.70 = f32[512,4096]{1,0:T(8,128)} fusion(bf16[512,1536]{1,0:T(8,128)(2,1)} %bitcast.262, bf16[4096,1536]{1,0:T(8,128)(2,1)} %all-gather.33.cloned.1.call-done), kind=kOutput, calls=%fused_computation.153 | convolution fusion | flops 6442450944 | bytes 22544384 | tf_op jit(solution)/shard_map/to,io->ti/dot_general | solution.py:77
  311.2 71.3 %all-gather.29.cloned.1.call-done = bf16[1536,4096]{1,0:T(8,128)(2,1)} async-done(((bf16[384,4096]{1,0:T(8,128)(2,1)}), bf16[1536,4096]{1,0:T(8,128)(2,1)}) %all-gather.29.cloned.1.call-update) | async-done | bytes 12582928 | tf_op jit(solution)/shard_map/all_gather | solution.py:226
  382.5 12.3 %fusion.68 = f32[512,4096]{1,0:T(8,128)} fusion(bf16[512,1536]{1,0:T(8,128)(2,1)} %copy-done.6, bf16[1536,4096]{1,0:T(8,128)(2,1)} %all-gather.29.cloned.1.call-done), kind=kOutput, calls=%fused_computation.151 | convolution fusion | flops 6442450944 | bytes 22544384 | tf_op jit(solution)/shard_map/dot_general | solution.py:67
  394.7 6.1 all-gather.35.cloned.1.call-done
  400.8 8.4 convolution_add_fusion
  409.2 9.8 all-gather.31.cloned.1.call-done
  419.0 8.5 convolution_add_fusion.1
  427.4 75.2 %all-gather.25.cloned.1.call-done = bf16[1536,4096]{1,0:T(8,128)(2,1)} async-done(((bf16[384,4096]{1,0:T(8,128)(2,1)}), bf16[1536,4096]{1,0:T(8,128)(2,1)}) %all-gather.25.cloned.1.call-update) | async-done | bytes 12582928 | tf_op jit(solution)/shard_map/all_gather | solution.py:225
  502.7 12.2 %fusion.67 = f32[512,4096]{1,0:T(8,128)} fusion(bf16[512,1536]{1,0:T(8,128)(2,1)} %copy-done.6, bf16[1536,4096]{1,0:T(8,128)(2,1)} %all-gather.25.cloned.1.call-done), kind=kOutput, calls=%fused_computation.150 | convolution fusion | flops 6442450944 | bytes 22544384 | tf_op jit(solution)/shard_map/dot_general | solution.py:67
  520.8 12.5 %multiply_convert_fusion.1 = (bf16[512,4096]{1,0:T(8,128)(2,1)S(1)}, bf16[512,4096]{1,0:T(8,128)(2,1)S(1)}, bf16[512,4096]{1,0:T(8,128)(2,1)}) fusion(f32[512,4096]{1,0:T(8,128)} %convolution_add_fusion, f32[512,4096]{1,0:T(8,128)} %convolution_add_fusion.1, f32[512,4096]{1,0:T(8,128)} %fusion.67, bf16[512,128]{1,0:T(8,128)(2,1)} %fusion.43, ...), kind=kOutput, calls=%fused_computation.15 | convolution fusion | flops 570425344 | bytes 38928384 | tf_op jit(solution)/shard_map/dot_general | solution.py:67
  533.4 12.2 %fusion.72 = f32[512,1536]{1,0:T(8,128)S(1)} fusion(bf16[512,4096]{1,0:T(8,128)(2,1)S(1)} %get-tuple-element.31, bf16[1536,4096]{1,0:T(8,128)(2,1)} %all-gather.29.cloned.1.call-done), kind=kOutput, calls=%fused_computation.155 | convolution fusion | flops 6442450944 | bytes 19922944 | tf_op jit(solution)/shard_map/to,io->ti/dot_general | solution.py:77
  547.6 9.7 fusion.71
  571.4 7.7 reshape.291
  585.1 23.1 %fusion = (f32[2,8,2,256]{3,2,1,0:T(2,128)S(1)}, f32[2,8,1024,256,2]{3,2,4,1,0:T(8,128)}) fusion(f32[2,8,2,256,1024]{3,4,2,1,0:T(8,128)} %get-tuple-element.48, f32[2,8,2,256]{3,2,1,0:T(2,128)S(1)} %bitcast.291, bf16[2,256,8,2,96]{1,4,3,2,0:T(8,128)(2,1)} %copy.89, bf16[2,1024,8,96]{1,3,2,0:T(8,128)(2,1)} %all-gather.15.cloned.1.call-done), kind=kOutput, calls=%fused_computation.2 | convolution fusion | flops 1635770368 | bytes 71892992 | tf_op jit(solution)/shard_map/sqkgd,sjkd->skgqj/dot_general | solution.py:117
  608.2 27.7 %fusion.2 = bf16[2,8,2,256,1024]{3,4,2,1,0:T(8,128)(2,1)} fusion(f32[2,8,1024,256,2]{3,2,4,1,0:T(8,128)} %get-tuple-element.54, f32[2,8,2,256,1024]{3,4,2,1,0:T(8,128)} %get-tuple-element.48, f32[2,8,2,256]{3,2,1,0:T(2,128)S(1)} %get-tuple-element.53, f32[2,8,2,256]{3,2,1,0:T(2,128)S(1)} %bitcast.292), kind=kLoop, calls=%fused_computation.4 | loop fusion | flops 33554432 | bytes 83951616 | tf_op jit(solution)/shard_map/convert_element_type | solution.py:122
  635.9 11.1 fusion.30
  654.1 6.7 add_convert_fusion
  693.0 15.8 %fusion.19 = bf16[2,1024,8,96]{1,3,2,0:T(8,128)(2,1)} fusion(bf16[2,256,8,2,96]{1,4,3,2,0:T(8,128)(2,1)} %copy.89, f32[2,8,2,256,1024]{3,4,2,1,0:T(8,128)} %get-tuple-element.48, f32[2,8,2,256]{3,2,1,0:T(2,128)S(1)} %bitcast.293), kind=kOutput, calls=%fused_computation.45 | convolution fusion | flops 1628962816 | bytes 38305792 | tf_op jit(solution)/shard_map/skgqj,sqkgd->sjkd/dot_general | solution.py:114
  708.9 10.5 fusion.18
  719.5 10.6 fusion.69
  731.9 6.7 fusion.73
  744.7 23.2 %reduce-scatter.39.cloned.1.call-done = bf16[384,128]{1,0:T(8,128)(2,1)} async-done(((bf16[1536,128]{1,0:T(8,128)(2,1)}), bf16[384,128]{1,0:T(8,128)(2,1)}) %reduce-scatter.39.cloned.1.call-update) | async-done | bytes 98320 | tf_op jit(solution)/shard_map/reduce_scatter | solution.py:380
  767.9 23.9 %reduce-scatter.27.cloned.1.call-done = bf16[384,128]{1,0:T(8,128)(2,1)} async-done(((bf16[1536,128]{1,0:T(8,128)(2,1)}), bf16[384,128]{1,0:T(8,128)(2,1)}) %reduce-scatter.27.cloned.1.call-update) | async-done | bytes 98320 | tf_op jit(solution)/shard_map/reduce_scatter | solution.py:356
  791.9 27.3 %reduce-scatter.41.cloned.1.call-done = bf16[128,1024]{1,0:T(8,128)(2,1)} async-done(((bf16[128,4096]{1,0:T(8,128)(2,1)}), bf16[128,1024]{1,0:T(8,128)(2,1)}) %reduce-scatter.41.cloned.1.call-update) | async-done | bytes 262160 | tf_op jit(solution)/shard_map/reduce_scatter | solution.py:383
  819.1 27.6 %reduce-scatter.45.cloned.1.call-done = bf16[128,1024]{1,0:T(8,128)(2,1)} async-done(((bf16[128,4096]{1,0:T(8,128)(2,1)}), bf16[128,1024]{1,0:T(8,128)(2,1)}) %reduce-scatter.45.cloned.1.call-update) | async-done | bytes 262160 | tf_op jit(solution)/shard_map/reduce_scatter | solution.py:389
  846.7 27.4 %reduce-scatter.47.cloned.1.call-done = bf16[1024,128]{1,0:T(8,128)(2,1)} async-done(((bf16[4096,128]{1,0:T(8,128)(2,1)}), bf16[1024,128]{1,0:T(8,128)(2,1)}) %reduce-scatter.47.cloned.1.call-update) | async-done | bytes 262160 | tf_op jit(solution)/shard_map/reduce_scatter | solution.py:392
  874.2 40.7 %reduce-scatter.25.cloned.1.call-done = bf16[2,256,8,96]{1,3,2,0:T(8,128)(2,1)} async-done(((bf16[2,1024,8,96]{1,3,2,0:T(8,128)(2,1)}), bf16[2,256,8,96]{1,3,2,0:T(8,128)(2,1)}) %reduce-scatter.25.cloned.1.call-update) | async-done | bytes 786448 | tf_op jit(solution)/shard_map/reduce_scatter | solution.py:304
  918.4 36.9 %reduce-scatter.23.cloned.1.call-done = bf16[2,256,8,96]{1,3,2,0:T(8,128)(2,1)} async-done(((bf16[2,1024,8,96]{1,3,2,0:T(8,128)(2,1)}), bf16[2,256,8,96]{1,3,2,0:T(8,128)(2,1)}) %reduce-scatter.23.cloned.1.call-update) | async-done | bytes 786448 | tf_op jit(solution)/shard_map/reduce_scatter | solution.py:301
  982.7 18.3 %reduce-scatter.31.cloned.1.call-done = bf16[128,192]{0,1:T(8,128)(2,1)} async-done(((bf16[128,768]{0,1:T(8,128)(2,1)}), bf16[128,192]{0,1:T(8,128)(2,1)}) %reduce-scatter.31.cloned.1.call-update) | async-done | bytes 49168 | tf_op jit(solution)/shard_map/reduce_scatter | solution.py:365
  1000.9 23.9 %reduce-scatter.33.cloned.1.call-done = bf16[384,128]{1,0:T(8,128)(2,1)} async-done(((bf16[1536,128]{1,0:T(8,128)(2,1)}), bf16[384,128]{1,0:T(8,128)(2,1)}) %reduce-scatter.33.cloned.1.call-update) | async-done | bytes 98320 | tf_op jit(solution)/shard_map/reduce_scatter | solution.py:368
  1024.8 24.1 %reduce-scatter.29.cloned.1.call-done = bf16[384,128]{1,0:T(8,128)(2,1)} async-done(((bf16[1536,128]{1,0:T(8,128)(2,1)}), bf16[384,128]{1,0:T(8,128)(2,1)}) %reduce-scatter.29.cloned.1.call-update) | async-done | bytes 98320 | tf_op jit(solution)/shard_map/reduce_scatter | solution.py:362
  1049.0 142.0 %all-reduce.2 = (f32[384,128]{1,0:T(8,128)}, f32[128,384]{1,0:T(8,128)}, f32[384,128]{1,0:T(8,128)}, f32[128,192]{0,1:T(8,128)}, f32[384,128]{1,0:T(8,128)}, /*i...) all-reduce(bf16[384,128]{1,0:T(8,128)(2,1)S(1)} %copy-done.85, ...), channel_id=1, replica_groups=mesh['rep'=8,'shard'=4] {'rep'}, use_global_device_ids=true, to_apply=%region_10.11 | all-reduce | flops 884736 | bytes 5308416 | tf_op jit(solution)/shard_map/psum | solution.py:399
  (377 shorter events, 176.4 us)
Async XLA Ops:
  7.2 30.2 %all-gather.17.cloned.1.call-start = ((), (), s32[]{:S(2)}) async-start(), calls=%async_computation.18 | async-start | bytes 2949120 | tf_op jit(solution)/shard_map/all_gather | solution.py:183
  8.0 61.9 %all-gather.13.cloned.1.call-start = ((), (), s32[]{:S(2)}) async-start(), calls=%async_computation.16 | async-start | bytes 2949120 | tf_op jit(solution)/shard_map/all_gather | solution.py:184
  8.7 136.5 %all-gather.21.cloned.1.call-start = ((), (), s32[]{:S(2)}) async-start(), calls=%async_computation.20 | async-start | bytes 5898240 | tf_op jit(solution)/shard_map/all_gather | solution.py:182
  9.4 150.1 %all-gather.19.cloned.1.call-start = ((), (), s32[]{:S(2)}) async-start(), calls=%async_computation.19 | async-start | bytes 3932160 | tf_op jit(solution)/shard_map/all_gather | solution.py:215
  18.6 126.6 %copy-start = (bf16[512,1536]{1,0:T(8,128)(2,1)}, bf16[512,1536]{1,0:T(8,128)(2,1)S(1)}, u32[]{:S(2)}) copy-start(bf16[512,1536]{1,0:T(8,128)(2,1)S(1)} %multiply_convert_fusion.4) | copy-start | bytes 4718596
  53.8 136.4 %all-gather.15.cloned.1.call-start = ((), (), s32[]{:S(2)}) async-start(), calls=%async_computation.17 | async-start | bytes 3932160 | tf_op jit(solution)/shard_map/all_gather | solution.py:216
  75.9 139.1 %all-gather.23.cloned.1.call-start = ((), (), s32[]{:S(2)}) async-start(), calls=%async_computation.21 | async-start | bytes 5898240 | tf_op jit(solution)/shard_map/all_gather | solution.py:185
  76.5 222.3 %all-gather.33.cloned.1.call-start = ((), (), s32[]{:S(2)}) async-start(), calls=%async_computation.26 | async-start | bytes 15728640 | tf_op jit(solution)/shard_map/all_gather | solution.py:227
  77.3 305.2 %all-gather.29.cloned.1.call-start = ((), (), s32[]{:S(2)}) async-start(), calls=%async_computation.24 | async-start | bytes 15728640 | tf_op jit(solution)/shard_map/all_gather | solution.py:226
  78.1 31.2 %copy-start.91 = (bf16[128,384]{1,0:T(8,128)(2,1)S(1)}, bf16[128,384]{1,0:T(8,128)(2,1)}, u32[]{:S(2)}) copy-start(bf16[128,384]{1,0:T(8,128)(2,1)} %param.47) | copy-start | bytes 294916
  78.1 38.0 %copy-start.92 = (bf16[384,128]{1,0:T(8,128)(2,1)S(1)}, bf16[384,128]{1,0:T(8,128)(2,1)}, u32[]{:S(2)}) copy-start(bf16[384,128]{1,0:T(8,128)(2,1)} %param.48) | copy-start | bytes 294916
  78.1 322.7 %all-gather.35.cloned.1.call-start = ((), (), s32[]{:S(2)}) async-start(), calls=%async_computation.27 | async-start | bytes 1310720 | tf_op jit(solution)/shard_map/all_gather | solution.py:232
  78.8 44.3 %copy-start.93 = (bf16[384,128]{1,0:T(8,128)(2,1)S(1)}, bf16[384,128]{1,0:T(8,128)(2,1)}, u32[]{:S(2)}) copy-start(bf16[384,128]{1,0:T(8,128)(2,1)} %param.50) | copy-start | bytes 294916
  78.8 340.1 %all-gather.31.cloned.1.call-start = ((), (), s32[]{:S(2)}) async-start(), calls=%async_computation.25 | async-start | bytes 1310720 | tf_op jit(solution)/shard_map/all_gather | solution.py:231
  79.4 53.2 %copy-start.94 = (bf16[128,384]{1,0:T(8,128)(2,1)S(1)}, bf16[128,384]{1,0:T(8,128)(2,1)}, u32[]{:S(2)}) copy-start(bf16[128,384]{1,0:T(8,128)(2,1)} %param.53) | copy-start | bytes 294916
  79.4 423.2 %all-gather.25.cloned.1.call-start = ((), (), s32[]{:S(2)}) async-start(), calls=%async_computation.22 | async-start | bytes 15728640 | tf_op jit(solution)/shard_map/all_gather | solution.py:225
  80.2 440.7 %all-gather.27.cloned.1.call-start = ((), (), s32[]{:S(2)}) async-start(), calls=%async_computation.23 | async-start | bytes 1310720 | tf_op jit(solution)/shard_map/all_gather | solution.py:229
  80.7 657.9 %reduce-scatter.51.cloned.1.call-start = ((), (), s32[]{:S(2)}) async-start(), calls=%async_computation.42 | async-start | bytes 491520
  81.1 62.9 %copy-start.10 = (bf16[2,256,1536]{2,1,0:T(8,128)(2,1)S(1)}, bf16[2,256,1536]{2,1,0:T(8,128)(2,1)}, u32[]{:S(2)}) copy-start(bf16[2,256,1536]{2,1,0:T(8,128)(2,1)} %param.28) | copy-start | bytes 4718596
  90.3 54.9 %copy-start.36 = (bf16[1536,128]{1,0:T(8,128)(2,1)}, bf16[1536,128]{1,0:T(8,128)(2,1)S(1)}, u32[]{:S(2)}) copy-start(bf16[1536,128]{1,0:T(8,128)(2,1)S(1)} %all_gather.99) | copy-start | bytes 1179652
  564.0 176.3 %reduce-scatter.53.cloned.1.call-start = ((), (), s32[]{:S(2)}) async-start(), calls=%async_computation.43 | async-start | bytes 491520
  654.0 87.9 %reduce-scatter.49.cloned.1.call-start = ((), (), s32[]{:S(2)}) async-start(), calls=%async_computation.41 | async-start | bytes 491520
  666.0 77.6 %reduce-scatter.37.cloned.1.call-start = ((), (), s32[]{:S(2)}) async-start(), calls=%async_computation.35 | async-start | bytes 491520 | tf_op jit(solution)/shard_map/reduce_scatter | solution.py:374
  668.8 75.9 %reduce-scatter.43.cloned.1.call-start = ((), (), s32[]{:S(2)}) async-start(), calls=%async_computation.38 | async-start | bytes 491520 | tf_op jit(solution)/shard_map/reduce_scatter | solution.py:386
  671.8 96.2 %reduce-scatter.39.cloned.1.call-start = ((), (), s32[]{:S(2)}) async-start(), calls=%async_computation.36 | async-start | bytes 491520 | tf_op jit(solution)/shard_map/reduce_scatter | solution.py:380
  674.6 117.2 %reduce-scatter.27.cloned.1.call-start = ((), (), s32[]{:S(2)}) async-start(), calls=%async_computation.30 | async-start | bytes 491520 | tf_op jit(solution)/shard_map/reduce_scatter | solution.py:356
  680.2 138.9 %reduce-scatter.41.cloned.1.call-start = ((), (), s32[]{:S(2)}) async-start(), calls=%async_computation.37 | async-start | bytes 1310720 | tf_op jit(solution)/shard_map/reduce_scatter | solution.py:383
  684.3 162.4 %reduce-scatter.45.cloned.1.call-start = ((), (), s32[]{:S(2)}) async-start(), calls=%async_computation.39 | async-start | bytes 1310720 | tf_op jit(solution)/shard_map/reduce_scatter | solution.py:389
  688.4 185.8 %reduce-scatter.47.cloned.1.call-start = ((), (), s32[]{:S(2)}) async-start(), calls=%async_computation.40 | async-start | bytes 1310720 | tf_op jit(solution)/shard_map/reduce_scatter | solution.py:392
  692.9 221.9 %reduce-scatter.25.cloned.1.call-start = ((), (), s32[]{:S(2)}) async-start(), calls=%async_computation.29 | async-start | bytes 3932160 | tf_op jit(solution)/shard_map/reduce_scatter | solution.py:304
  708.9 246.4 %reduce-scatter.23.cloned.1.call-start = ((), (), s32[]{:S(2)}) async-start(), calls=%async_computation.28 | async-start | bytes 3932160 | tf_op jit(solution)/shard_map/reduce_scatter | solution.py:301
  719.4 263.2 %reduce-scatter.35.cloned.1.call-start = ((), (), s32[]{:S(2)}) async-start(), calls=%async_computation.34 | async-start | bytes 245760 | tf_op jit(solution)/shard_map/reduce_scatter | solution.py:371
  738.6 178.4 %copy-start.62 = (bf16[512,128]{1,0:T(8,128)(2,1)S(1)}, bf16[512,128]{1,0:T(8,128)(2,1)}, u32[]{:S(2)}) copy-start(bf16[512,128]{1,0:T(8,128)(2,1)} %copy-done.61) | copy-start | bytes 393220
  743.6 213.0 %copy-start.45 = (f32[256,48]{0,1:T(8,128)S(1)}, f32[256,48]{0,1:T(8,128)}, u32[]{:S(2)}) copy-start(f32[256,48]{0,1:T(8,128)} %copy-done.43) | copy-start | bytes 147460
  743.6 213.0 %copy-start.48 = (f32[256,48]{0,1:T(8,128)S(1)}, f32[256,48]{0,1:T(8,128)}, u32[]{:S(2)}) copy-start(f32[256,48]{0,1:T(8,128)} %copy-done.46) | copy-start | bytes 147460
  918.1 82.9 %reduce-scatter.31.cloned.1.call-start = ((), (), s32[]{:S(2)}) async-start(), calls=%async_computation.32 | async-start | bytes 245760 | tf_op jit(solution)/shard_map/reduce_scatter | solution.py:365
  961.9 62.9 %reduce-scatter.33.cloned.1.call-start = ((), (), s32[]{:S(2)}) async-start(), calls=%async_computation.33 | async-start | bytes 491520 | tf_op jit(solution)/shard_map/reduce_scatter | solution.py:368
  967.4 81.5 %reduce-scatter.29.cloned.1.call-start = ((), (), s32[]{:S(2)}) async-start(), calls=%async_computation.31 | async-start | bytes 491520 | tf_op jit(solution)/shard_map/reduce_scatter | solution.py:362
  977.2 71.7 %copy-start.72 = (bf16[128,384]{1,0:T(8,128)(2,1)S(1)}, bf16[128,384]{1,0:T(8,128)(2,1)}, u32[]{:S(2)}) copy-start(bf16[128,384]{1,0:T(8,128)(2,1)} %copy.111) | copy-start | bytes 294916
  977.3 71.6 %copy-start.73 = (bf16[128,384]{1,0:T(8,128)(2,1)S(1)}, bf16[128,384]{1,0:T(8,128)(2,1)}, u32[]{:S(2)}) copy-start(bf16[128,384]{1,0:T(8,128)(2,1)} %copy.113) | copy-start | bytes 294916
  977.3 71.6 %copy-start.74 = (bf16[128,384]{1,0:T(8,128)(2,1)S(1)}, bf16[128,384]{1,0:T(8,128)(2,1)}, u32[]{:S(2)}) copy-start(bf16[128,384]{1,0:T(8,128)(2,1)} %copy.109) | copy-start | bytes 294916
  977.3 71.6 %copy-start.77 = (bf16[128,1024]{1,0:T(8,128)(2,1)S(1)}, bf16[128,1024]{1,0:T(8,128)(2,1)}, u32[]{:S(2)}) copy-start(bf16[128,1024]{1,0:T(8,128)(2,1)} %reduce-scatter.41.cloned.1.call-done) | copy-start | bytes 786436
  977.3 71.6 %copy-start.78 = (bf16[128,1024]{1,0:T(8,128)(2,1)S(1)}, bf16[128,1024]{1,0:T(8,128)(2,1)}, u32[]{:S(2)}) copy-start(bf16[128,1024]{1,0:T(8,128)(2,1)} %reduce-scatter.45.cloned.1.call-done) | copy-start | bytes 786436
  977.3 71.6 %copy-start.79 = (bf16[1024,128]{1,0:T(8,128)(2,1)S(1)}, bf16[1024,128]{1,0:T(8,128)(2,1)}, u32[]{:S(2)}) copy-start(bf16[1024,128]{1,0:T(8,128)(2,1)} %reduce-scatter.47.cloned.1.call-done) | copy-start | bytes 786436
  977.3 71.6 %copy-start.82 = (bf16[384,128]{1,0:T(8,128)(2,1)S(1)}, bf16[384,128]{1,0:T(8,128)(2,1)}, u32[]{:S(2)}) copy-start(bf16[384,128]{1,0:T(8,128)(2,1)} %reduce-scatter.37.cloned.1.call-done) | copy-start | bytes 294916
  977.3 71.6 %copy-start.83 = (bf16[384,128]{1,0:T(8,128)(2,1)S(1)}, bf16[384,128]{1,0:T(8,128)(2,1)}, u32[]{:S(2)}) copy-start(bf16[384,128]{1,0:T(8,128)(2,1)} %reduce-scatter.43.cloned.1.call-done) | copy-start | bytes 294916
  977.3 71.6 %copy-start.84 = (bf16[384,128]{1,0:T(8,128)(2,1)S(1)}, bf16[384,128]{1,0:T(8,128)(2,1)}, u32[]{:S(2)}) copy-start(bf16[384,128]{1,0:T(8,128)(2,1)} %reduce-scatter.39.cloned.1.call-done) | copy-start | bytes 294916
  977.3 71.6 %copy-start.85 = (bf16[384,128]{1,0:T(8,128)(2,1)S(1)}, bf16[384,128]{1,0:T(8,128)(2,1)}, u32[]{:S(2)}) copy-start(bf16[384,128]{1,0:T(8,128)(2,1)} %reduce-scatter.27.cloned.1.call-done) | copy-start | bytes 294916
  (85 other events, 503.0 us)
Sparse Core Ops, SparseCore 0:
  9.6 27.8 all-gather.16
  39.0 26.1 all-gather.12
  66.8 43.7 all-gather.20
  112.6 33.1 all-gather.18
  147.2 28.9 all-gather.14
  177.6 37.4 all-gather.22
  216.6 82.0 all-gather.32
  300.3 82.0 all-gather.28
  384.0 16.7 all-gather.34
  402.2 16.7 all-gather.30
  420.5 82.0 all-gather.24
  504.1 16.7 all-gather.26
  564.1 20.7 reduce-scatter.50
  654.1 20.8 reduce-scatter.52
  677.3 20.8 reduce-scatter.48
  700.6 20.9 reduce-scatter.36
  723.9 20.7 reduce-scatter.42
  747.0 20.8 reduce-scatter.38
  771.0 20.8 reduce-scatter.26
  794.2 24.8 reduce-scatter.40
  821.8 24.8 reduce-scatter.44
  849.3 24.8 reduce-scatter.46
  876.9 37.9 reduce-scatter.24
  917.3 37.9 reduce-scatter.22
  958.4 19.7 reduce-scatter.34
  981.2 19.6 reduce-scatter.30
  1004.0 20.7 reduce-scatter.32
  1028.0 20.7 reduce-scatter.28
where the time goes:
time: 1210 us; the launch traced here: 1200 us
  waiting for transfers between devices  540 us (45%)
  matrix products  284 us (23%)
  blocking collectives  232 us (19%)
  other arithmetic  65.1 us (5%)
  local copies, waits for them, and re-layouts  59.3 us (5%)
  between operations  16.5 us (1%)
    psum x1, blocking collectives, local(): lax.psum((owned[0], owned[1], owned[2], owned[3], owned[4], owned[5], own...  142 us
    all_gather x1, waiting for transfers between devices, local(): lax.all_gather(gate_weight, 'shard', axis=0, tiled=True)  75.2 us
    all_gather x1, waiting for transfers between devices, local(): lax.all_gather(drop_weight, 'shard', axis=0, tiled=True)  74 us
    all_gather x1, waiting for transfers between devices, local(): lax.all_gather(lift_weight, 'shard', axis=0, tiled=True)  71.3 us
    dot_general x7, matrix products, project_back(): jnp.einsum('to,io->ti', out_grad, weight, preferred_element_type=jnp.floa...  53 us
    dot_general x7, matrix products, project(): jnp.dot(source, weight, preferred_element_type=jnp.float32)  50.5 us
    reduce_scatter x1, waiting for transfers between devices, local(): lax.psum_scatter(value_full_grad.astype(jnp.bfloat16), 'shard', scatter_d...  40.7 us
    reduce_scatter x1, waiting for transfers between devices, local(): lax.psum_scatter(key_full_grad.astype(jnp.bfloat16), 'shard', scatter_dim...  36.9 us
  transfers between devices with their start and end apart: 28, of which 19 were waited for; matrix products, arithmetic and copies ran while one was open for 30% of the time, Pallas kernels for 0%

commit v1 on v0

v1 whole, which is shorter than its diff:
```python
import functools
import math
from typing import NamedTuple

import jax
import jax.numpy as jnp
from jax import lax
from jax.experimental import pallas as pl
from jax.experimental.pallas import tpu as pltpu
from jax.sharding import PartitionSpec as P

HEADS = 16
KV_HEADS = 8
HEAD_DIM = 96
RANK = 16
ADAPTERS = 8
EPSILON = 1e-05
ROPE_BASE = 100000.0
MASKED_SCORE = -1e30
AXES = ("rep", "shard")
F32 = jnp.float32
BF16 = jnp.bfloat16


def move(value, target):
    reps, shards = lax.axis_size("rep"), lax.axis_size("shard")
    pairs = []
    for r in range(reps):
        for s in range(shards):
            r2, s2 = target(r, s)
            pairs.append((r * shards + s, r2 * shards + s2))
    return lax.ppermute(value, AXES, pairs)


def to_core(value):
    return move(value, lambda r, s: (r, s ^ 1))


def to_chip(value):
    return move(value, lambda r, s: (r, s ^ 2))


def to_diag(value):
    return move(value, lambda r, s: (r, s ^ 3))


def to_y(value):
    return move(value, lambda r, s: (r ^ 1, s))


def to_z(value):
    return move(value, lambda r, s: (r ^ 2, s))


PANEL = 512


class Piece(NamedTuple):
    parts: tuple
    row: int
    rows: int
    target: int
    block: int
    to_row: int
    to_col: int


class Bundle(NamedTuple):
    first: tuple
    second: tuple
    shapes: tuple


def quarter_rows(pieces):
    return sum(p.rows for p in pieces) // 4


def make_bundles(width, kv_width, ff, chunks, shards):
    rows, drop_rows = width // shards, ff // shards // chunks
    panels = width // PANEL
    first = tuple(Piece(((0, c, PANEL),), 0, rows, 0, rows, 0, c) for c in range(0, width, PANEL))
    second = []
    for c in range(0, 2 * kv_width, PANEL):
        parts, at = [], c
        while at < c + PANEL:
            source = 1 if at < kv_width else 2
            base = (source - 1) * kv_width
            stop = min(c + PANEL, base + kv_width)
            parts.append((source, at - base, stop - at))
            at = stop
        second.append(Piece(tuple(parts), 0, rows, 0, rows, 0, width + c))
    found = [Bundle(first, tuple(second), ((width, width + 2 * kv_width),))]

    def halves(source, row, height, target, block):
        return [
            tuple(
                Piece(((source, i * PANEL, PANEL),), row + h * height // 2, height // 2, target, block,
                      h * height // 2, i * PANEL)
                for i in range(panels)
            )
            for h in range(2)
        ]

    top, bottom = halves(3, 0, rows, 0, rows)
    found.append(Bundle(top, bottom, ((width, width),)))
    part = ff // shards // chunks
    for u in range(chunks):
        sides = []
        for j in range(2):
            side = []
            for c in range(0, shards * part, PANEL):
                parts = tuple(
                    (4 + j, t * (ff // shards) + u * part, part)
                    for t in range(c // part, (c + PANEL) // part)
                )
                side.append(Piece(parts, 0, rows, 0, rows, 0, 2 * c + j * PANEL))
            sides.append(tuple(side))
        top, bottom = halves(6, u * drop_rows, drop_rows, 1, drop_rows)
        cols = shards * part
        found.append(
            Bundle(sides[0] + top, sides[1] + bottom, ((width, 2 * cols), (cols, width)))
        )
    return found


def run_copies(copies, sems):
    started = []
    for i, (src, dst) in enumerate(copies):
        started.append(pltpu.make_async_copy(src, dst, sems.at[i]))
        started[-1].start()
    for c in started:
        c.wait()


def pack(place, jobs, operands, out_shapes, name):
    count = []

    def kernel(place_ref, *refs):
        ins, outs, sems = refs[: len(operands)], refs[len(operands) : -1], refs[-1]
        run_copies(jobs(place_ref, ins, outs), sems)

    class Fake:
        def __init__(self):
            self.at = self

        def __getitem__(self, _):
            return self

    count = len(jobs(None, [Fake()] * len(operands), [Fake()] * len(out_shapes)))
    return pl.pallas_call(
        kernel,
        out_shape=[jax.ShapeDtypeStruct(sh, BF16) for sh in out_shapes],
        grid_spec=pltpu.PrefetchScalarGridSpec(
            num_scalar_prefetch=1,
            grid=(1,),
            in_specs=[pl.BlockSpec(memory_space=pl.ANY)] * len(operands),
            out_specs=[pl.BlockSpec(memory_space=pltpu.VMEM)] * len(out_shapes),
            scratch_shapes=[pltpu.SemaphoreType.DMA((count,))],
        ),
        compiler_params=pltpu.CompilerParams(vmem_limit_bytes=40 * 2**20),
        name=name,
    )(place, *operands)


def quarter_start(place_ref, flip, rows):
    if place_ref is None:
        return 0
    return pl.multiple_of((place_ref[1] ^ flip) * rows, 16)


class Relay:
    def __init__(self, place, weights, bundles):
        self.place, self.weights, self.bundles = place, weights, bundles
        self.direct, self.once, self.twice = {}, {}, {}
        self.far, self.far_near = {}, {}
        self.tick = 0

    def step(self, extra=(), ties=()):
        t, bundles = self.tick, self.bundles
        self.tick += 1
        operands, shapes, kinds = [], [], []

        def operand(array):
            for i, o in enumerate(operands):
                if o is array:
                    return i
            operands.append(array)
            return len(operands) - 1

        plans = []

        def out(kind, rows, cols=PANEL):
            shapes.append((rows, cols))
            kinds.append(kind)
            return len(shapes) - 1

        if t < len(bundles):
            b = bundles[t]
            o = out("x", quarter_rows(b.first + b.second))
            used = [(operand(self.weights[q[0]]), q, p) for p in b.first + b.second for q in p.parts]

            def plan_x(pr, ins, outs, o=o, used=used):
                copies, at, col = [], 0, 0
                for i, (_, c, n), p in used:
                    q = p.rows // 4
                    rows = pl.ds(pl.multiple_of(p.row + quarter_start(pr, 0, q), 16), q)
                    copies.append((ins[i].at[rows, pl.ds(c, n)],
                                   outs[o].at[pl.ds(at, q), pl.ds(col, n)]))
                    col += n
                    if col == PANEL:
                        at, col = at + q, 0
                return copies

            plans.append(plan_x)
        y_parts, z_parts = [], []
        b1, b2, b3 = t - 1, t - 2, t - 3
        if 0 <= b1 < len(bundles):
            qa, qb = quarter_rows(bundles[b1].first), quarter_rows(bundles[b1].second)
            y_parts.append(("first", b1, [(self.direct[b1], 0, qa)]))
            z_parts.append(("first", b1, [(self.direct[b1], qa, qb)]))
        if 0 <= b2 < len(bundles):
            qa, qb = quarter_rows(bundles[b2].first), quarter_rows(bundles[b2].second)
            (ya, yo), (za, zo) = self.once[b2]
            y_parts.append(("second", b2, [(self.direct[b2], qa, qb), (za, zo, qb)]))
            z_parts.append(("second", b2, [(self.direct[b2], 0, qa), (ya, yo, qa)]))
        for kind, parts in (("y", y_parts), ("z", z_parts)):
            if not parts:
                continue
            total = sum(n for _, _, l in parts for _, _, n in l)
            o = out(kind, total)
            flat = [(operand(a), r, n) for _, _, l in parts for a, r, n in l]

            def plan_n(pr, ins, outs, o=o, flat=flat):
                copies, at = [], 0
                for i, r, n in flat:
                    copies.append((ins[i].at[pl.ds(r, n)], outs[o].at[pl.ds(at, n)]))
                    at += n
                return copies

            plans.append(plan_n)
        if 0 <= b3 < len(bundles):
            b = bundles[b3]
            o = out("c", 4 * quarter_rows(b.first + b.second))
            qa = quarter_rows(b.first)
            qb = quarter_rows(b.second)
            (ya, yo), (za, zo) = self.once[b3]
            (ys, yso), (zs, zso) = self.twice[b3]
            d = operand(self.direct[b3])
            sides = [
                (b.first, [(0, d, 0), (1, operand(ya), yo), (2, operand(zs), zso), (3, operand(zs), zso + qa)]),
                (b.second, [(0, d, qa), (2, operand(za), zo), (1, operand(ys), yso), (3, operand(ys), yso + qb)]),
            ]

            def plan_c(pr, ins, outs, o=o, sides=sides):
                copies, base = [], 0
                for pieces, quarters in sides:
                    at = 0
                    for p in pieces:
                        q = p.rows // 4
                        for flip, i, r in quarters:
                            to = pl.multiple_of(base + quarter_start(pr, flip, q), 16)
                            copies.append((ins[i].at[pl.ds(r + at, q)], outs[o].at[pl.ds(to, q)]))
                        at += q
                        base += p.rows
                return copies

            plans.append(plan_c)
        for array, index in extra:
            o = out("d", array.shape[1], array.shape[2])
            i = operand(array)

            def plan_d(pr, ins, outs, o=o, i=i, index=index):
                which = 0 if pr is None else index(pr)
                return [(ins[i].at[which], outs[o])]

            plans.append(plan_d)
        for tie in ties:
            operand(tie)

        def jobs(pr, ins, outs):
            return [c for plan in plans for c in plan(pr, ins, outs)]

        bufs = pack(self.place, jobs, operands, shapes, f"pack_{t}")
        sent = []
        for kind, buf in zip(kinds, bufs):
            if kind == "x":
                self.direct[t] = to_chip(buf)
            elif kind == "c":
                self.far[b3], self.far_near[b3] = buf, to_core(buf)
            elif kind == "d":
                sent.append(to_diag(buf))
            else:
                got = (to_y if kind == "y" else to_z)(buf)
                at = 0
                for stage, bi, l in y_parts if kind == "y" else z_parts:
                    store = self.once if stage == "first" else self.twice
                    pair = store.setdefault(bi, [None, None])
                    pair[0 if kind == "y" else 1] = (got, at)
                    at += sum(n for _, _, n in l)
        return sent, bufs


def land_copies(place_ref, bundle, own, near, far, far_near, targets):
    copies = []
    shard = 0 if place_ref is None else place_ref[0]
    for slot, refs in enumerate((own, near, far, far_near)):
        base = 0
        for p in bundle.first + bundle.second:
            to = (shard ^ slot) * p.block + p.to_row
            to = pl.ds(pl.multiple_of(to, 16), p.rows)
            dst = targets[p.target]
            if slot < 2:
                col = p.to_col
                for source, c, n in p.parts:
                    copies.append((refs[source].at[pl.ds(p.row, p.rows), pl.ds(c, n)],
                                   dst.at[to, pl.ds(col, n)], (p.target, p.to_col, slot)))
                    col += n
            else:
                copies.append((refs.at[pl.ds(base, p.rows)], dst.at[to, pl.ds(p.to_col, PANEL)],
                               (p.target, p.to_col, slot)))
            base += p.rows
    return copies


def sources_of(bundle):
    return sorted({q[0] for p in bundle.first + bundle.second for q in p.parts})


def rotary_tables(positions, head_dim):
    half_dim = head_dim // 2
    freq_index = jnp.arange(half_dim).astype(F32)
    frequency = jnp.exp(freq_index * (-2.0 * math.log(ROPE_BASE) / head_dim))
    angles = positions[:, None] * frequency[None, :]
    return jnp.cos(angles), jnp.sin(angles)


def dot(left, right):
    return jnp.dot(left, right, preferred_element_type=F32)


def dot_nt(left, right):
    return lax.dot_general(left, right, (((1,), (1,)), ((), ())), preferred_element_type=F32)


def dot_tn(left, right):
    return lax.dot_general(left, right, (((0,), (0,)), ((), ())), preferred_element_type=F32)


LOG2E = 1.4426950408889634


def last_visible(place_ref, low, lanes, block):
    shard, prefix = place_ref[0], place_ref[2]
    low_block = (shard ^ (shard // 2)) & 1
    at = low_block if low else 3 - low_block
    position = at * block + lax.broadcasted_iota(jnp.int32, (1, lanes), 1) % block
    return jnp.maximum(position + 1, prefix)


def query_start(place_ref, low, block):
    chip = place_ref[0] // 2
    return pl.multiple_of((chip if low else 1 - chip) * block, block)


def natural_rows(place_ref, own, near, into, block):
    shard = place_ref[0]
    for slot, value in (
        (0, own[0, :block]),
        (3, own[0, block:]),
        (1, near[0, :block]),
        (2, near[0, block:]),
    ):
        into[pl.ds(pl.multiple_of((shard ^ slot) * block, block), block)] = value


def hide(scores, limit, first_key):
    keys = first_key + lax.broadcasted_iota(jnp.int32, scores.shape, 0)
    return jnp.where(keys < limit, scores, MASKED_SCORE)


def masked_by_part(low, scores, limit, block):
    if low:
        return hide(scores, limit, 0)
    half = 2 * block
    return jnp.concatenate([scores[:half], hide(scores[half:], limit, half)], axis=0)


def attend_kernel(place, q, k_own, k_near, v_own, v_near, out, lse, keys, values, *, scale):
    block = q.shape[1] // 2
    group = q.shape[0]
    natural_rows(place, k_own, k_near, keys, block)
    natural_rows(place, v_own, v_near, values, block)
    values_t = values[...].T
    for part, low in enumerate((True, False)):
        count = (2 if low else 4) * block
        rows = pl.ds(query_start(place, low, block), block)
        query = jnp.concatenate([q[j, rows] for j in range(group)], axis=0)
        limit = last_visible(place, low, group * block, block)
        scores = masked_by_part(low, dot_nt(keys[:count], query), limit, block)
        top = jnp.max(scores, axis=0, keepdims=True)
        base = scale * LOG2E
        expo = jnp.exp2(scores * base - top * base)
        total = jnp.sum(expo, axis=0, keepdims=True)
        lse[0, part] = (top * base + jnp.log2(total))[0]
        result = dot(values_t[:, :count], expo.astype(BF16)) / total
        result = result.T.astype(BF16)
        for j in range(group):
            out[j, rows] = result[j * block : (j + 1) * block]


def attend(place, queries, k_own, k_near, v_own, v_near):
    heads, rows, dim = queries.shape
    kv_heads = k_own.shape[0]
    group = heads // kv_heads
    q_spec = pl.BlockSpec((group, rows, dim), lambda g, p: (g, 0, 0))
    kv_spec = pl.BlockSpec((1, rows, dim), lambda g, p: (g, 0, 0))
    lse_shape = (kv_heads, 2, group * rows // 2)
    return pl.pallas_call(
        functools.partial(attend_kernel, scale=dim ** (-0.5)),
        out_shape=[
            jax.ShapeDtypeStruct(queries.shape, BF16),
            jax.ShapeDtypeStruct(lse_shape, F32),
        ],
        grid_spec=pltpu.PrefetchScalarGridSpec(
            num_scalar_prefetch=1,
            grid=(kv_heads,),
            in_specs=[q_spec] + [kv_spec] * 4,
            out_specs=[q_spec, pl.BlockSpec((1, *lse_shape[1:]), lambda g, p: (g, 0, 0))],
            scratch_shapes=[pltpu.VMEM((2 * rows, dim), BF16)] * 2,
        ),
        compiler_params=pltpu.CompilerParams(vmem_limit_bytes=40 * 2**20),
        name="attend",
    )(place, queries, k_own, k_near, v_own, v_near)


def attend_back_kernel(
    place, q, k_own, k_near, v_own, v_near, grad, lse, cos_t, sin_t,
    dq, dk_own, dk_send, dv_own, dv_send, keys, values, dk, dv, *, scale
):
    block = q.shape[1] // 2
    group = q.shape[0]
    half = q.shape[2] // 2
    natural_rows(place, k_own, k_near, keys, block)
    natural_rows(place, v_own, v_near, values, block)
    keys_t = keys[...].T
    for part, low in ((1, False), (0, True)):
        count = (2 if low else 4) * block
        start = query_start(place, low, block)
        rows = pl.ds(start, block)
        query = jnp.concatenate([q[j, rows] for j in range(group)], axis=0)
        out_grad = jnp.concatenate([grad[j, rows] for j in range(group)], axis=0)
        limit = last_visible(place, low, group * block, block)
        scores = masked_by_part(low, dot_nt(keys[:count], query), limit, block)
        probs = jnp.exp2(scores * (scale * LOG2E) - lse[0, part][None])
        probs_grad = dot_nt(values[:count], out_grad)
        mean = jnp.sum(probs * probs_grad, axis=0, keepdims=True)
        score_grad = (probs * (probs_grad - mean)).astype(BF16)
        v_part = dot(probs.astype(BF16), out_grad)
        k_part = dot(score_grad, query) * scale
        if low:
            dk[:count] += k_part
            dv[:count] += v_part
        else:
            dk[...] = k_part
            dv[...] = v_part
        turned = dot(keys_t[:, :count], score_grad) * scale
        cos = jnp.concatenate([cos_t[:, rows]] * group, axis=1)
        sin = jnp.concatenate([sin_t[:, rows]] * group, axis=1)
        u, w = turned[:half], turned[half:]
        turned = jnp.concatenate([u * cos + w * sin, w * cos - u * sin], axis=0)
        turned = turned.T.astype(BF16)
        for j in range(group):
            dq[j, rows] = turned[j * block : (j + 1) * block]
    shard = place[0]
    for slot, at, own in ((0, 0, True), (3, 1, True), (1, 0, False), (2, 1, False)):
        rows = pl.ds(pl.multiple_of((shard ^ slot) * block, block), block)
        to = slice(at * block, (at + 1) * block)
        (dk_own if own else dk_send)[0, to] = dk[rows].astype(F32 if own else BF16)
        (dv_own if own else dv_send)[0, to] = dv[rows].astype(F32 if own else BF16)


def attend_back(place, queries, k_own, k_near, v_own, v_near, grad, lse, cos_t, sin_t):
    heads, rows, dim = queries.shape
    kv_heads = k_own.shape[0]
    group = heads // kv_heads
    q_spec = pl.BlockSpec((group, rows, dim), lambda g, p: (g, 0, 0))
    kv_spec = pl.BlockSpec((1, rows, dim), lambda g, p: (g, 0, 0))
    whole = pl.BlockSpec(cos_t.shape, lambda g, p: (0, 0))
    return pl.pallas_call(
        functools.partial(attend_back_kernel, scale=dim ** (-0.5)),
        out_shape=[
            jax.ShapeDtypeStruct(queries.shape, BF16),
            jax.ShapeDtypeStruct(k_own.shape, F32),
            jax.ShapeDtypeStruct(k_own.shape, BF16),
            jax.ShapeDtypeStruct(k_own.shape, F32),
            jax.ShapeDtypeStruct(k_own.shape, BF16),
        ],
        grid_spec=pltpu.PrefetchScalarGridSpec(
            num_scalar_prefetch=1,
            grid=(kv_heads,),
            in_specs=[q_spec] + [kv_spec] * 4
            + [q_spec, pl.BlockSpec((1, *lse.shape[1:]), lambda g, p: (g, 0, 0)), whole, whole],
            out_specs=[q_spec] + [kv_spec] * 4,
            scratch_shapes=[pltpu.VMEM((2 * rows, dim), BF16)] * 2
            + [pltpu.VMEM((2 * rows, dim), F32)] * 2,
        ),
        compiler_params=pltpu.CompilerParams(vmem_limit_bytes=40 * 2**20),
        name="attend_back",
    )(place, queries, k_own, k_near, v_own, v_near, grad, lse, cos_t, sin_t)


class Landing:
    def __init__(self, place, bundle, refs, targets, sems):
        used = sources_of(bundle)
        n = len(used)
        own, near = dict(zip(used, refs[:n])), dict(zip(used, refs[n : 2 * n]))
        listed = land_copies(place, bundle, own, near, refs[2 * n], refs[2 * n + 1], targets)
        self.copies = [
            (key, pltpu.make_async_copy(src, dst, sems.at[i])) for i, (src, dst, key) in enumerate(listed)
        ]
        self.copies.sort(key=lambda c: c[0])
        for _, c in self.copies:
            c.start()

    def wait(self, wanted=None):
        left = []
        for key, c in self.copies:
            if wanted is None or wanted(key):
                c.wait()
            else:
                left.append((key, c))
        self.copies = left


def landing_operands(bundle, weights, near, far, far_near):
    used = sources_of(bundle)
    return [weights[i] for i in used] + [near[i] for i in used] + [far, far_near]


def landing_count(bundle):
    return sum(2 * len(p.parts) + 2 for p in bundle.first + bundle.second)


def kernel_call(body, place, bundle, landing, operands, outs, scratch, name, aliases=None, flops=0):
    n_land, n_in, n_out, n_w = len(landing), len(operands), len(outs), len(bundle.shapes)

    def kernel(place_ref, *refs):
        land, refs = refs[:n_land], refs[n_land:]
        ins, refs = refs[:n_in], refs[n_in:]
        out, refs = refs[:n_out], refs[n_out:]
        body(place_ref, land, ins, out, refs[:n_w], refs[n_w], refs[n_w + 1 :])

    def spec(where):
        return pl.BlockSpec(memory_space=where)

    return pl.pallas_call(
        kernel,
        out_shape=[o for o, _ in outs],
        grid_spec=pltpu.PrefetchScalarGridSpec(
            num_scalar_prefetch=1,
            grid=(1,),
            in_specs=[spec(pl.ANY)] * n_land + [spec(w) for _, w in operands],
            out_specs=[spec(w) for _, w in outs],
            scratch_shapes=[pltpu.VMEM(sh, BF16) for sh in bundle.shapes]
            + [pltpu.SemaphoreType.DMA((landing_count(bundle),))]
            + list(scratch),
        ),
        input_output_aliases={1 + n_land + i: o for i, o in (aliases or {}).items()},
        compiler_params=pltpu.CompilerParams(vmem_limit_bytes=58 * 2**20),
        cost_estimate=pl.CostEstimate(flops=flops, bytes_accessed=20 * 2**20, transcendentals=0),
        name=name,
    )(place, *landing, *[a for a, _ in operands])


VM = pltpu.VMEM


def like(shape, dtype):
    return jax.ShapeDtypeStruct(shape, dtype)


def turn(value, cos_full, sin_signed, half):
    swapped = jnp.concatenate([value[:, half:], value[:, :half]], axis=1)
    return value * cos_full + swapped * sin_signed


def qkv_forward(place, bundle, landing, tokens_kept, tokens_back, gain, inner, outer, cos, sin):
    block, width = tokens_kept.shape
    rows = 2 * block
    total = bundle.shapes[0][1]
    kv = (total - width) // 2
    wide = 8 * HEAD_DIM
    half = HEAD_DIM // 2

    def body(pr, land_refs, ins, outs, weights, sems, scratch):
        kept, back, gain_ref, inner_ref, outer_ref, cos_ref, sin_ref = ins
        q, k, v, hidden_ref, normed_ref, x_ref = outs
        (w,) = weights
        landing = Landing(pr, bundle, land_refs, weights, sems)
        x_ref[:block] = kept[...]
        x_ref[block:] = back[...]
        x = x_ref[...].astype(F32)
        scale = lax.rsqrt(jnp.mean(x * x, axis=-1, keepdims=True) + EPSILON)
        normed_ref[...] = (x * scale * gain_ref[...].astype(F32)).astype(BF16)
        hidden_ref[...] = dot_nt(normed_ref[...], inner_ref[...]).astype(BF16)

        def columns(at):
            cols = pl.ds(at, wide)
            return dot(normed_ref[...], w[:, cols]) + dot(hidden_ref[...], outer_ref[:, cols])

        landing.wait(lambda key: key[1] < width)
        for i in range(width // wide):
            acc = columns(i * wide)
            for h in range(8):
                one = acc[:, h * HEAD_DIM : (h + 1) * HEAD_DIM]
                q[8 * i + h] = turn(one, cos_ref[...], sin_ref[...], half).astype(BF16)
        landing.wait()
        acc = columns(width)
        for h in range(8):
            one = acc[:, h * HEAD_DIM : (h + 1) * HEAD_DIM]
            k[h] = turn(one, cos_ref[...], sin_ref[...], half).astype(BF16)
        acc = columns(width + kv)
        for h in range(8):
            v[h] = acc[:, h * HEAD_DIM : (h + 1) * HEAD_DIM].astype(BF16)

    heads = width // HEAD_DIM
    return kernel_call(
        body, place, bundle, landing,
        [(tokens_kept, VM), (tokens_back, VM), (gain, VM), (inner, VM), (outer, VM), (cos, VM), (sin, VM)],
        [
            (like((heads, rows, HEAD_DIM), BF16), VM),
            (like((kv // HEAD_DIM, rows, HEAD_DIM), BF16), VM),
            (like((kv // HEAD_DIM, rows, HEAD_DIM), BF16), VM),
            (like((rows, inner.shape[0]), BF16), VM),
            (like((rows, width), BF16), VM),
            (like((rows, width), BF16), VM),
        ],
        [], "qkv_forward", flops=2 * rows * width * total,
    )


def out_forward(place, bundle, landing, heads_out, x, gain, inner, outer):
    rows, width = x.shape
    heads = heads_out.shape[0]

    def body(pr, land_refs, ins, outs, weights, sems, scratch):
        heads_ref, x_ref, gain_ref, inner_ref, outer_ref = ins
        middle, normed, attended, hidden = outs
        landing = Landing(pr, bundle, land_refs, weights, sems)
        for h in range(heads):
            attended[:, h * HEAD_DIM : (h + 1) * HEAD_DIM] = heads_ref[h]
        hidden[...] = dot_nt(attended[...], inner_ref[...]).astype(BF16)
        landing.wait()
        wide = width // 2
        squares = jnp.zeros((rows, 1), F32)
        for i in range(2):
            cols = pl.ds(i * wide, wide)
            branch = dot(attended[...], weights[0][:, cols]) + dot(hidden[...], outer_ref[:, cols])
            value = x_ref[:, cols].astype(F32) + branch
            middle[:, cols] = value
            squares += jnp.sum(value * value, axis=-1, keepdims=True)
        scale = lax.rsqrt(squares / width + EPSILON)
        normed[...] = (middle[...] * scale * gain_ref[...].astype(F32)).astype(BF16)

    return kernel_call(
        body, place, bundle, landing,
        [(heads_out, VM), (x, VM), (gain, VM), (inner, VM), (outer, VM)],
        [
            (like((rows, width), F32), VM),
            (like((rows, width), BF16), VM),
            (like((rows, width), BF16), VM),
            (like((rows, RANK), BF16), VM),
        ],
        [], "out_forward", flops=2 * rows * width * width,
    )


def mlp_chunk(place, bundle, landing, normed, cot, inner_gl, outer_gl, drop_a, drop_b, sums, name):
    rows, width = normed.shape
    units = bundle.shapes[1][0]
    steps = units // PANEL
    first = sums is None

    def body(pr, land_refs, ins, outs, weights, sems, scratch):
        normed_ref, cot_ref, igl, ogl, da, db = ins[:6]
        drop_sum, e_sum, thin, g_gate, g_lift, g_drop = outs
        w_gl, w_d = weights
        landing = Landing(pr, bundle, land_refs, weights, sems)
        h_gl = dot_nt(normed_ref[...], igl[...]).astype(BF16)
        h_d = dot_nt(cot_ref[...], db[...]).astype(BF16)
        h_g, h_l = h_gl[:, :RANK], h_gl[:, RANK:]
        g_t, l_t, d_t = h_g.T, h_l.T, h_d.T
        for i in range(steps):
            landing.wait(lambda key: key[0] == 1 or key[1] < 2 * (i + 1) * PANEL)
            cols = slice(i * PANEL, (i + 1) * PANEL)
            both = pl.ds(2 * i * PANEL, 2 * PANEL)
            acts = dot(normed_ref[...], w_gl[:, both])
            gate = acts[:, :PANEL] + dot(h_g, ogl[:RANK, cols])
            lift = acts[:, PANEL:] + dot(h_l, ogl[RANK:, cols])
            a_grad = dot_nt(cot_ref[...], w_d[cols]) + dot(h_d, da[:, cols])
            sig = 1.0 / (1.0 + jnp.exp(-gate))
            silu = gate * sig
            active = (silu * lift).astype(BF16)
            gate_grad = (a_grad * lift * sig * (1.0 + gate * (1.0 - sig))).astype(BF16)
            lift_grad = (a_grad * silu).astype(BF16)
            grads = jnp.concatenate([gate_grad, lift_grad], axis=1)
            down = dot(active, w_d[cols])
            back = dot_nt(grads, w_gl[:, both])
            t0 = dot_nt(active, da[:, cols])
            t1 = dot_nt(gate_grad, ogl[:RANK, cols])
            t2 = dot_nt(lift_grad, ogl[RANK:, cols])
            if i == 0 and first:
                drop_sum[...] = down
                e_sum[...] = back
                thin[0], thin[1], thin[2] = t0, t1, t2
            elif i == 0:
                drop_sum[...] = ins[6][...] + down
                e_sum[...] = ins[7][...] + back
                thin[0], thin[1], thin[2] = ins[8][0] + t0, ins[8][1] + t1, ins[8][2] + t2
            else:
                drop_sum[...] += down
                e_sum[...] += back
                thin[0] += t0
                thin[1] += t1
                thin[2] += t2
            g_gate[:, cols] = dot(g_t, gate_grad)
            g_lift[:, cols] = dot(l_t, lift_grad)
            g_drop[:, cols] = dot(d_t, active)

    operands = [(normed, VM), (cot, VM), (inner_gl, VM), (outer_gl, VM), (drop_a, VM), (drop_b, VM)]
    if not first:
        operands += [(s, VM) for s in sums]
    return kernel_call(
        body, place, bundle, landing, operands,
        [
            (like((rows, width), F32), VM),
            (like((rows, width), F32), VM),
            (like((3, rows, RANK), F32), VM),
            (like((RANK, units), F32), VM),
            (like((RANK, units), F32), VM),
            (like((RANK, units), F32), VM),
        ],
        [], name, flops=12 * rows * width * units,
    )


def out_backward(place, bundle, landing, sums, middle, cot, gain, normed, attended, hidden, factors):
    rows, width = middle.shape
    heads = width // HEAD_DIM

    def body(pr, land_refs, ins, outs, weights, sems, scratch):
        drop_sum, e_sum, thin, middle_ref, cot_ref, gain_ref, normed_ref, att, hid, drop_b, igl, o_a, o_b = ins
        mixed, mid_grad, branch, out_heads, g_drop, g_gl, g_oa, g_ob = outs
        (w,) = weights
        landing = Landing(pr, bundle, land_refs, weights, sems)
        d_hid = thin[0].astype(BF16)
        gl_grad = jnp.concatenate([thin[1].astype(BF16), thin[2].astype(BF16)], axis=1)
        e_in = (e_sum[...] + dot(gl_grad, igl[...])) * gain_ref[...].astype(F32)
        mid = middle_ref[...]
        scale = lax.rsqrt(jnp.mean(mid * mid, axis=-1, keepdims=True) + EPSILON)
        n = mid * scale
        mean = jnp.mean(e_in * n, axis=-1, keepdims=True)
        mid_grad[...] = cot_ref[...].astype(F32) + scale * (e_in - n * mean)
        branch[...] = mid_grad[...].astype(BF16)
        hgrad = dot_nt(branch[...], o_b[...]).astype(BF16)
        landing.wait()
        wide = 8 * HEAD_DIM
        for i in range(heads // 8):
            part = slice(i * wide, (i + 1) * wide)
            grad = dot_nt(branch[...], w[part]) + dot(hgrad, o_a[:, part])
            for h in range(8):
                out_heads[8 * i + h] = grad[:, h * HEAD_DIM : (h + 1) * HEAD_DIM].astype(BF16)
        mixed[...] = (mid + drop_sum[...] + dot(d_hid, drop_b[...])).astype(BF16)
        g_drop[...] = dot(d_hid.T, cot_ref[...])
        g_gl[...] = dot(gl_grad.T, normed_ref[...])
        g_oa[...] = dot(hgrad.T, att[...])
        g_ob[...] = dot(hid[...].T, branch[...])

    thin_shape = (like((RANK, width), F32), VM)
    return kernel_call(
        body, place, bundle, landing,
        [(v, VM) for v in (*sums, middle, cot, gain, normed, attended, hidden, *factors)],
        [
            (like((rows, width), BF16), VM),
            (like((rows, width), F32), VM),
            (like((rows, width), BF16), VM),
            (like((heads, rows, HEAD_DIM), BF16), VM),
            thin_shape,
            (like((2 * RANK, width), F32), VM),
            thin_shape,
            thin_shape,
        ],
        [], "out_backward", flops=2 * rows * width * width,
    )


def qkv_backward(place, bundle, landing, dq, dk, dv, cos, sin, x, mid_grad, gain, normed, hidden, inner, outer):
    rows, width = x.shape
    total = bundle.shapes[0][1]
    kv = (total - width) // 2
    half = HEAD_DIM // 2
    block = rows // 2

    def body(pr, land_refs, ins, outs, weights, sems, scratch):
        dq_ref, dk_ref, dk_got, dv_ref, dv_got, cos_ref, sin_ref, x_ref, mg, gain_ref, nrm, hid, a, b = ins
        kept, back, g_inner, g_outer = outs
        (w,) = weights
        (g,) = scratch
        landing = Landing(pr, bundle, land_refs, weights, sems)
        for h in range(width // HEAD_DIM):
            g[:, h * HEAD_DIM : (h + 1) * HEAD_DIM] = dq_ref[h]
        for h in range(kv // HEAD_DIM):
            one = dk_ref[h] + dk_got[h].astype(F32)
            at = width + h * HEAD_DIM
            g[:, at : at + HEAD_DIM] = turn(one, cos_ref[...], -sin_ref[...], half).astype(BF16)
            at += kv
            g[:, at : at + HEAD_DIM] = (dv_ref[h] + dv_got[h].astype(F32)).astype(BF16)
        hgrad = dot_nt(g[...], b[...]).astype(BF16)
        g_inner[...] = dot(hgrad.T, nrm[...])
        g_outer[...] = dot(hid[...].T, g[...])
        landing.wait()
        e_in = (dot_nt(g[...], w[...]) + dot(hgrad, a[...])) * gain_ref[...].astype(F32)
        xf = x_ref[...].astype(F32)
        scale = lax.rsqrt(jnp.mean(xf * xf, axis=-1, keepdims=True) + EPSILON)
        n = xf * scale
        mean = jnp.mean(e_in * n, axis=-1, keepdims=True)
        result = mg[...] + scale * (e_in - n * mean)
        kept[...] = result[:block]
        back[...] = result[block:].astype(BF16)

    return kernel_call(
        body, place, bundle, landing,
        [(v, VM) for v in (dq, *dk, *dv, cos, sin, x, mid_grad, gain, normed, hidden, inner, outer)],
        [
            (like((block, width), F32), VM),
            (like((block, width), BF16), VM),
            (like((inner.shape[0], width), F32), VM),
            (like((inner.shape[0], total), F32), VM),
        ],
        [pltpu.VMEM((rows, total), BF16)], "qkv_backward", flops=2 * rows * width * total,
    )


def local(
    tokens,
    cotangent,
    prefix_len,
    adapter_index,
    gain_attn,
    gain_mlp,
    query_weight,
    key_weight,
    value_weight,
    output_weight,
    gate_weight,
    lift_weight,
    drop_weight,
    *factors,
):
    _, block, width = tokens.shape
    rep, shard = lax.axis_index("rep"), lax.axis_index("shard")
    chip, core = shard // 2, shard % 2
    member = rep % 4
    place = jnp.stack([shard, member, prefix_len[chip]]).astype(jnp.int32)
    rows = 2 * block
    kv_width = KV_HEADS * HEAD_DIM

    def pick(pair, index):
        return lax.dynamic_index_in_dim(pair, index, 0, keepdims=False)

    def swap_out(kept, back, dtype):
        back = to_diag(back.astype(BF16)).astype(dtype)
        return jnp.where(chip == 0, jnp.stack([kept, back]), jnp.stack([back, kept]))

    inners, outers = factors[0::2], factors[1::2]
    widths = [a.shape[0] for a in inners] + [b.shape[1] for b in outers]

    def pack(sequence):
        at = adapter_index[sequence] * RANK
        parts = [lax.dynamic_slice_in_dim(a, at, RANK, 1).T for a in inners]
        parts += [lax.dynamic_slice_in_dim(b, at, RANK, 0) for b in outers]
        return jnp.concatenate(parts, axis=1)

    mine = pack(chip)
    slot_two = to_chip(pack(1 - chip))
    slots = jnp.stack([mine, to_core(mine), slot_two, to_core(slot_two)])
    packed = jnp.take(slots, shard ^ jnp.arange(4), axis=0)
    factor_list, at = [], 0
    for w in widths:
        factor_list.append(
            packed[:, :, at : at + w].transpose(1, 0, 2).reshape(RANK, 4 * w)
        )
        at += w
    inner_t, outer = factor_list[:7], factor_list[7:]

    weights = (query_weight, key_weight, value_weight, output_weight, gate_weight, lift_weight, drop_weight)
    chunks = 4
    ff = gate_weight.shape[1]
    bundles = make_bundles(width, kv_width, ff, chunks, 4)
    near = [to_core(w) for w in weights]
    relay = Relay(place, weights, bundles)
    other_pair = lambda pr: 1 - pr[0] // 2
    relay.step()
    (tokens_back,), _ = relay.step([(tokens, other_pair)])
    relay.step()
    relay.step()
    (cot_back,), _ = relay.step([(cotangent, other_pair)])
    cot = jnp.concatenate([pick(cotangent, chip), cot_back], axis=0)
    for _ in range(len(bundles) - 2):
        relay.step()

    def landing(i):
        return landing_operands(bundles[i], weights, near, relay.far[i], relay.far_near[i])

    positions = jnp.concatenate(
        [shard * block + jnp.arange(block), (shard ^ 3) * block + jnp.arange(block)]
    )
    cos_table, sine_table = rotary_tables(positions.astype(F32), HEAD_DIM)
    cos_full = jnp.concatenate([cos_table, cos_table], axis=1)
    sin_full = jnp.concatenate([-sine_table, sine_table], axis=1)
    gain_one, gain_two = gain_attn[None], gain_mlp[None]

    inner_qkv = jnp.concatenate(inner_t[:3], axis=0)
    zeros = lambda w: jnp.zeros((RANK, w), BF16)
    outer_qkv = jnp.concatenate(
        [
            jnp.concatenate([outer[0], zeros(2 * kv_width)], axis=1),
            jnp.concatenate([zeros(width), outer[1], zeros(kv_width)], axis=1),
            jnp.concatenate([zeros(width + kv_width), outer[2]], axis=1),
        ],
        axis=0,
    )
    queries, k_own, v_own, hidden_qkv, normed_attn, x = qkv_forward(
        place, bundles[0], landing(0), pick(tokens, chip), tokens_back, gain_one,
        inner_qkv, outer_qkv, cos_full, sin_full,
    )
    k_near, v_near = to_core(k_own), to_core(v_own)
    heads_out, lse = attend(place, queries, k_own, k_near, v_own, v_near)
    middle, normed_mlp, attended, output_hidden = out_forward(
        place, bundles[1], landing(1), heads_out, x, gain_two, inner_t[3], outer[3]
    )

    def chunk_of(factor, i):
        return factor.reshape(factor.shape[0], 4, chunks, -1)[:, :, i].reshape(factor.shape[0], -1)

    def whole_of(parts):
        return jnp.stack([p.reshape(RANK, 4, -1) for p in parts], axis=2).reshape(RANK, -1)

    inner_gl = jnp.concatenate([inner_t[4], inner_t[5]], axis=0)
    outer_gl = jnp.concatenate([outer[4], outer[5]], axis=0)
    sums, grads_mlp = None, []
    for u in range(chunks):
        *sums, gg, gl, gd = mlp_chunk(
            place, bundles[2 + u], landing(2 + u), normed_mlp, cot, inner_gl,
            chunk_of(outer_gl, u), chunk_of(inner_t[6], u), outer[6], sums, f"mlp_{u}",
        )
        grads_mlp.append((gg, gl, gd))
    gate_outer_grad, lift_outer_grad, drop_inner_grad = map(whole_of, zip(*grads_mlp))
    mixed, middle_grad, branch_grad, grad_heads, drop_outer_grad, gl_inner, output_inner_grad, output_outer_grad = (
        out_backward(
            place, bundles[1], landing(1), sums, middle, cot, gain_two, normed_mlp, attended, output_hidden,
            (outer[6], inner_gl, inner_t[3], outer[3]),
        )
    )
    gate_inner_grad, lift_inner_grad = gl_inner[:RANK], gl_inner[RANK:]
    mixed = swap_out(mixed[:block], mixed[block:], BF16)

    column_owner = jnp.arange(ADAPTERS * RANK)

    def reduce_grads(inner_list, outer_list):
        parts = [v.reshape(RANK, 4, -1).transpose(1, 0, 2) for v in inner_list + outer_list]
        widths_here = [v.shape[2] for v in parts]
        everything = jnp.concatenate(parts, axis=2)
        keep = jnp.take(everything, core + jnp.array([0, 2]), axis=0)
        send = jnp.take(everything, (core ^ 1) + jnp.array([0, 2]), axis=0)
        summed = keep + to_core(send.astype(BF16)).astype(F32)
        own = pick(summed, chip).astype(BF16)
        other = to_chip(pick(summed, 1 - chip).astype(BF16))
        both = jnp.concatenate([own, other], axis=0)
        ids = jnp.stack([adapter_index[chip], adapter_index[1 - chip]])
        tag = jnp.broadcast_to(jnp.repeat(ids, RANK)[:, None], (2 * RANK, 128)).astype(BF16)
        gathered = lax.all_gather(jnp.concatenate([both, tag], axis=1), "rep", axis=0, tiled=True)
        owner = gathered[:, -1].astype(jnp.int32) * RANK + jnp.arange(gathered.shape[0]) % RANK
        choose = (column_owner[:, None] == owner[None, :]).astype(BF16)
        total = dot(choose, gathered[:, :-128])
        out, at = [], 0
        for w in widths_here:
            out.append(total[:, at : at + w])
            at += w
        n = len(inner_list)
        return [v.T for v in out[:n]], out[n:]

    inner_late, outer_late = reduce_grads(
        [output_inner_grad, gate_inner_grad, lift_inner_grad, drop_inner_grad],
        [output_outer_grad, gate_outer_grad, lift_outer_grad, drop_outer_grad],
    )

    dq, dk_own, dk_send, dv_own, dv_send = attend_back(
        place, queries, k_own, k_near, v_own, v_near, grad_heads, lse, cos_table.T, sine_table.T
    )
    input_kept, input_back, g_inner, g_outer = qkv_backward(
        place, bundles[0], landing(0), dq, (dk_own, to_core(dk_send)), (dv_own, to_core(dv_send)),
        cos_full, sin_full, x, middle_grad, gain_one, normed_attn, hidden_qkv, inner_qkv, outer_qkv,
    )
    input_grad = swap_out(input_kept, input_back, F32)
    stops = (0, width, width + kv_width, width + 2 * kv_width)
    inner_first, outer_first = reduce_grads(
        [g_inner[i * RANK : (i + 1) * RANK] for i in range(3)],
        [g_outer[i * RANK : (i + 1) * RANK, stops[i] : stops[i + 1]] for i in range(3)],
    )
    inner_out = inner_first + inner_late
    outer_out = outer_first + outer_late
    grads = [g for pair in zip(inner_out, outer_out) for g in pair]
    return (mixed, input_grad, *grads)


def solution(mesh):
    token_place = P("rep", "shard", None)
    row, col = P("shard", None), P(None, "shard")
    return jax.shard_map(
        local,
        mesh=mesh,
        in_specs=(token_place, token_place, P("rep"), P("rep"), P(), P()) + (row,) * 7 + (row, col) * 7,
        out_specs=(token_place, token_place) + (row, col) * 7,
        check_vma=False,
    )
```

time: 1210 us -> 643 us (0.53)
  waiting for transfers between devices: 540 us -> 176 us
  matrix products: 284 us -> 3.75 us
  blocking collectives: 232 us -> 0 us
  Pallas kernels: 0 us -> 227 us
  local copies, waits for them, and re-layouts: 59.3 us -> 154 us
  other arithmetic: 65.1 us -> 21.3 us
  starting transfers between devices: 1.38 us -> 33.6 us
    dot_general x62 -> x2, matrix products: 284 us -> 3.75 us  [dot(): return jnp.dot(left, right, preferred_element_type=F32)]
    reduce_scatter x13 -> x0, waiting for transfers between devices: 274 us -> none  [the longest x1 40.7 us: local(): lax.psum_scatter(value_full_grad.astype(jnp.bfloat16), 'shard', scatter_d...]
    pallas_call x0 -> x19, Pallas kernels: none -> 227 us  [the longest x8 158 us: kernel_call(): pl.pallas_call(kernel, out_shape=[o for o, _ in outs], grid_spec=pltpu.Pr...]
    all_gather x12 -> x2, waiting for transfers between devices: 259 us -> 44.1 us  [reduce_grads(): lax.all_gather(jnp.concatenate([both, tag], axis=1), 'rep', axis=0, tiled...]
    psum x1 -> x0, blocking collectives: 142 us -> none  [local(): lax.psum((owned[0], owned[1], owned[2], owned[3], owned[4], owned[5], own...]
    ppermute x0 -> x48, waiting for transfers between devices: none -> 132 us  [move(): return lax.ppermute(value, AXES, pairs)]
    all_gather x11 -> x0, blocking collectives: 89.9 us -> none  [the longest x1 9.51 us: local(): lax.all_gather(query_outer, 'shard', axis=1, tiled=True)]
    unnamed x223 -> x179, local copies, waits for them, and re-layouts: 21.1 us -> 71 us
  transfers between devices with their start and end apart: 28 -> 50, of which waited for: 19 -> 19; matrix products, arithmetic and copies ran while one was open for 30% -> 19% of each run, Pallas kernels for 0% -> 22%
where the time goes in v1:
time: 643 us; the launch traced here: 634 us
  Pallas kernels  227 us (35%)
  waiting for transfers between devices  176 us (27%)
  local copies, waits for them, and re-layouts  154 us (24%)
  starting transfers between devices  33.6 us (5%)
  other arithmetic  21.3 us (3%)
  between operations  18 us (3%)
    pallas_call x8, Pallas kernels, kernel_call(): pl.pallas_call(kernel, out_shape=[o for o, _ in outs], grid_spec=pltpu.Pr...  158 us
    ppermute x48, waiting for transfers between devices, move(): return lax.ppermute(value, AXES, pairs)  132 us
    unnamed x179, local copies, waits for them, and re-layouts  71 us
    all_gather x2, waiting for transfers between devices, reduce_grads(): lax.all_gather(jnp.concatenate([both, tag], axis=1), 'rep', axis=0, tiled...  44.1 us
    pallas_call x9, Pallas kernels, pack(): pl.pallas_call(kernel, out_shape=[jax.ShapeDtypeStruct(sh, BF16) for sh i...  33.6 us
    ppermute x48, starting transfers between devices, move(): return lax.ppermute(value, AXES, pairs)  33.4 us
    pallas_call x1, Pallas kernels, attend_back(): pl.pallas_call(functools.partial(attend_back_kernel, scale=dim ** (-0.5))...  20.9 us
    another operation x24, local copies, waits for them, and re-layouts, whole_of(): jnp.stack([p.reshape(RANK, 4, -1) for p in parts], axis=2).reshape(RANK, -1)  16.9 us
  transfers between devices with their start and end apart: 50, of which 19 were waited for; matrix products, arithmetic and copies ran while one was open for 19% of the time, Pallas kernels for 22%

profile of v1, /device:TPU:0, one launch (start us, length us, event | category | flops | bytes accessed | tf_op | source)
XLA Modules:
  0.0 633.8 jit_solution(1712772700248499109)
XLA Ops:
  13.1 3.0 collective-permute-start.1
  16.1 13.3 %collective-permute-done.1.refs_1_.refs_4_.refs_7_ = bf16[576,512]{1,0:T(8,128)(2,1)S(1)} collective-permute-done((bf16[576,512]{1,0:T(8,128)(2,1)S(1)}, bf16[576,512]{1,0:T(8,128)(2,1)S(1)}, u32[]{:S(2)}, u32[]{:S(2)}) %collective-permute-start.1) | collective-permute-done | bytes 589856 | tf_op jit(solution)/shard_map/ppermute | solution.py:32
  29.5 1.8 pack_1.1
  39.1 2.1 constant_dynamic-slice_fusion.21
  44.2 3.6 pack_2.1
  59.5 1.9 constant_dynamic-slice_fusion.22
  77.6 5.3 pack_3.1
  99.9 2.2 dynamic-slice_bitcast_fusion.1.refs_8_
  102.1 4.0 pack_4.1
  115.5 10.8 %collective-permute-done.15.refs_3_.refs_1_ = bf16[576,512]{1,0:T(8,128)(2,1)} collective-permute-done((bf16[576,512]{1,0:T(8,128)(2,1)}, bf16[576,512]{1,0:T(8,128)(2,1)}, u32[]{:S(2)}, u32[]{:S(2)}) %collective-permute-start.15) | collective-permute-done | bytes 589856 | tf_op jit(solution)/shard_map/ppermute | solution.py:32
  126.3 5.0 collective-permute-done.16.refs_5_.refs_6_
  131.3 2.2 pad_maximum_fusion.1
  133.5 2.7 gather_fusion
  136.7 5.3 pack_5.1
  149.0 12.8 %collective-permute-done.18.refs_0_ = bf16[576,512]{1,0:T(8,128)(2,1)} collective-permute-done((bf16[576,512]{1,0:T(8,128)(2,1)}, bf16[576,512]{1,0:T(8,128)(2,1)}, u32[]{:S(2)}, u32[]{:S(2)}) %collective-permute-start.18) | collective-permute-done | bytes 589856 | tf_op jit(solution)/shard_map/ppermute | solution.py:32
  161.7 4.1 collective-permute-done.19.refs_2_.refs_5_
  169.0 4.2 pack_6.1
  174.6 7.1 %collective-permute-done.30.refs_9_ = bf16[256,1536]{1,0:T(8,128)(2,1)S(1)} collective-permute-done((bf16[256,1536]{1,0:T(8,128)(2,1)}, bf16[256,1536]{1,0:T(8,128)(2,1)S(1)}, u32[]{:S(2)}, u32[]{:S(2)}) %collective-permute-start.30) | collective-permute-done | bytes 786464 | tf_op jit(solution)/shard_map/ppermute | solution.py:32
  181.7 16.4 %collective-permute-done.36 = bf16[256,1536]{1,0:T(8,128)(2,1)S(1)} collective-permute-done((bf16[256,1536]{1,0:T(8,128)(2,1)}, bf16[256,1536]{1,0:T(8,128)(2,1)S(1)}, u32[]{:S(2)}, u32[]{:S(2)}) %collective-permute-start.36) | collective-permute-done | bytes 786464 | tf_op jit(solution)/shard_map/ppermute | solution.py:32
  201.0 15.5 %qkv_forward.1 = (bf16[16,512,96]{2,1,0:T(8,128)(2,1)}, bf16[8,512,96]{2,1,0:T(8,128)(2,1)}, bf16[8,512,96]{2,1,0:T(8,128)(2,1)}, bf16[512,48]{1,0:T(8,128)(2,1)...) custom-call(s32[3]{0:T(128)} %copy-done.28, bf16[384,1536]{1,0:T(8,128)(2,1)} %refs_0_.27, ...), custom_call_target="tpu_custom_call" | custom-call | flops 4831838208 | bytes 20971520 | tf_op jit(solution)/shard_map/qkv_forward/pallas_call | solution.py:556
  216.5 2.4 copy.167
  224.8 2.7 pack_7.1
  237.2 7.4 %collective-permute-done.23.refs_2_ = bf16[576,512]{1,0:T(8,128)(2,1)S(1)} collective-permute-done((bf16[576,512]{1,0:T(8,128)(2,1)S(1)}, bf16[576,512]{1,0:T(8,128)(2,1)S(1)}, u32[]{:S(2)}, u32[]{:S(2)}) %collective-permute-start.23) | collective-permute-done | bytes 589856 | tf_op jit(solution)/shard_map/ppermute | solution.py:32
  247.2 12.2 %collective-permute-done.24.refs_4_ = bf16[576,512]{1,0:T(8,128)(2,1)S(1)} collective-permute-done((bf16[576,512]{1,0:T(8,128)(2,1)S(1)}, bf16[576,512]{1,0:T(8,128)(2,1)S(1)}, u32[]{:S(2)}, u32[]{:S(2)}) %collective-permute-start.24) | collective-permute-done | bytes 589856 | tf_op jit(solution)/shard_map/ppermute | solution.py:32
  273.5 2.2 copy.170.v_near
  278.6 14.6 %attend.1 = (bf16[16,512,96]{2,1,0:T(8,128)(2,1)S(1)}, f32[8,2,512]{2,1,0:T(2,128)S(1)}) custom-call(s32[3]{0:T(128)S(1)} %copy-done.29, bf16[16,512,96]{2,1,0:T(8,128)(2,1)S(1)} %copy-done.5, bf16[8,512,96]{2,1,0:T(8,128)(2,1)S(1)} %copy-done.1, bf16[8,512,96]{2,1,0:T(8,128)(2,1)S(1)} %copy.169.k_near, bf16[8,512,96]{2,1,0:T(8,128)(2,1)S(1)} %copy-done.2, ...), custom_call_target="tpu_custom_call" | custom-call | tf_op jit(solution)/shard_map/attend/pallas_call | solution.py:418
  294.6 12.3 %out_forward.1 = (f32[512,1536]{1,0:T(8,128)}, bf16[512,1536]{1,0:T(8,128)(2,1)}, bf16[512,1536]{1,0:T(8,128)(2,1)}, bf16[512,16]{1,0:T(8,128)(2,1)}) custom-call(s32[3]{0:T(128)} %copy-done.28, bf16[384,1536]{1,0:T(8,128)(2,1)} %refs_0_.26, bf16[384,1536]{1,0:T(8,128)(2,1)} %copy-done.44, bf16[1152,512]{1,0:T(8,128)(2,1)} %copy-done.20, ...), custom_call_target="tpu_custom_call" | custom-call | flops 2415919104 | bytes 20971520 | tf_op jit(solution)/shard_map/out_forward/pallas_call | solution.py:556
  309.0 5.2 pack_8.1.refs_6_
  314.8 21.7 %mlp_0.1 = (f32[512,1536]{1,0:T(8,128)}, f32[512,1536]{1,0:T(8,128)}, f32[3,512,16]{2,1,0:T(8,128)}, f32[16,1024]{1,0:T(8,128)}, f32[16,1024]{1,0:T(8,128)}, /*index=5*/f32[16,1024]{1,0:T(8,128)}) custom-call(s32[3]{0:T(128)} %copy-done.28, bf16[384,4096]{1,0:T(8,128)(2,1)} %refs_0_.25, bf16[384,4096]{1,0:T(8,128)(2,1)} %refs_1_.20, ...), custom_call_target="tpu_custom_call" | custom-call | flops 9663676416 | bytes 20971520 | tf_op jit(solution)/shard_map/mlp_0/pallas_call | solution.py:556
  340.6 24.2 %mlp_1.1 = (f32[512,1536]{1,0:T(8,128)}, f32[512,1536]{1,0:T(8,128)}, f32[3,512,16]{2,1,0:T(8,128)}, f32[16,1024]{1,0:T(8,128)}, f32[16,1024]{1,0:T(8,128)}, /*index=5*/f32[16,1024]{1,0:T(8,128)}) custom-call(s32[3]{0:T(128)} %copy-done.28, bf16[384,4096]{1,0:T(8,128)(2,1)} %refs_0_.25, bf16[384,4096]{1,0:T(8,128)(2,1)} %refs_1_.20, ...), custom_call_target="tpu_custom_call" | custom-call | flops 9663676416 | bytes 20971520 | tf_op jit(solution)/shard_map/mlp_1/pallas_call | solution.py:556
  369.5 24.0 %mlp_2.1 = (f32[512,1536]{1,0:T(8,128)}, f32[512,1536]{1,0:T(8,128)}, f32[3,512,16]{2,1,0:T(8,128)}, f32[16,1024]{1,0:T(8,128)}, f32[16,1024]{1,0:T(8,128)}, /*index=5*/f32[16,1024]{1,0:T(8,128)}) custom-call(s32[3]{0:T(128)} %copy-done.28, bf16[384,4096]{1,0:T(8,128)(2,1)} %refs_0_.25, bf16[384,4096]{1,0:T(8,128)(2,1)} %refs_1_.20, ...), custom_call_target="tpu_custom_call" | custom-call | flops 9663676416 | bytes 20971520 | tf_op jit(solution)/shard_map/mlp_2/pallas_call | solution.py:556
  398.2 24.0 %mlp_3.1 = (f32[512,1536]{1,0:T(8,128)}, f32[512,1536]{1,0:T(8,128)}, f32[3,512,16]{2,1,0:T(8,128)}, f32[16,1024]{1,0:T(8,128)}, f32[16,1024]{1,0:T(8,128)}, /*index=5*/f32[16,1024]{1,0:T(8,128)}) custom-call(s32[3]{0:T(128)} %copy-done.28, bf16[384,4096]{1,0:T(8,128)(2,1)} %refs_0_.25, bf16[384,4096]{1,0:T(8,128)(2,1)} %refs_1_.20, ...), custom_call_target="tpu_custom_call" | custom-call | flops 9663676416 | bytes 20971520 | tf_op jit(solution)/shard_map/mlp_3/pallas_call | solution.py:556
  423.1 1.9 pad_maximum_fusion.7
  425.0 1.8 reshape_reshape.18
  429.2 1.9 pad_maximum_fusion.5
  431.1 1.8 reshape_reshape.16
  432.9 14.6 %out_backward.1 = (bf16[512,1536]{1,0:T(8,128)(2,1)}, f32[512,1536]{1,0:T(8,128)}, bf16[512,1536]{1,0:T(8,128)(2,1)}, bf16[16,512,96]{2,1,0:T(8,128)(2,1)}, f32[...) custom-call(s32[3]{0:T(128)} %copy-done.28, bf16[384,1536]{1,0:T(8,128)(2,1)} %refs_0_.26, ...), custom_call_target="tpu_custom_call" | custom-call | flops 2415919104 | bytes 20971520 | tf_op jit(solution)/shard_map/out_backward/pallas_call | solution.py:556
  450.7 20.9 %attend_back.1 = (bf16[16,512,96]{2,1,0:T(8,128)(2,1)S(1)}, f32[8,512,96]{2,1,0:T(8,128)S(1)}, bf16[8,512,96]{2,1,0:T(8,128)(2,1)S(1)}, f32[8,512,96]{2,1,0:T(8,128)S(1)}, bf16[8,512,96]{2,1,0:T(8,128)(2,1)S(1)}) custom-call(s32[3]{0:T(128)S(1)} %copy-done.31, bf16[16,512,96]{2,1,0:T(8,128)(2,1)} %get-tuple-element.118.q, bf16[8,512,96]{2,1,0:T(8,128)(2,1)S(1)} %copy-done.1, ...), custom_call_target="tpu_custom_call" | custom-call | tf_op jit(solution)/shard_map/attend_back/pallas_call | solution.py:489
  485.0 2.2 copy.186.refs_10_
  487.2 2.6 copy.187.refs_12_
  489.8 21.6 %qkv_backward.1 = (f32[256,1536]{1,0:T(8,128)}, bf16[256,1536]{1,0:T(8,128)(2,1)}, f32[48,1536]{1,0:T(8,128)}, f32[48,3072]{1,0:T(8,128)}) custom-call(s32[3]{0:T(128)} %copy-done.28, bf16[384,1536]{1,0:T(8,128)(2,1)} %refs_0_.27, bf16[384,768]{1,0:T(8,128)(2,1)} %refs_1_.21, bf16[384,768]{1,0:T(8,128)(2,1)} %refs_2_.23, ...), custom_call_target="tpu_custom_call" | custom-call | flops 4831838208 | bytes 20971520 | tf_op jit(solution)/shard_map/qkv_backward/pallas_call | solution.py:556
  518.4 2.7 collective-permute-done.45
  523.1 4.6 collective-permute-done.47
  530.4 18.1 %collective-permute-done.40 = bf16[256,1536]{1,0:T(8,128)(2,1)S(1)} collective-permute-done((bf16[256,1536]{1,0:T(8,128)(2,1)S(1)}, bf16[256,1536]{1,0:T(8,128)(2,1)S(1)}, u32[]{:S(2)}, u32[]{:S(2)}) %collective-permute-start.40) | collective-permute-done | bytes 786464 | tf_op jit(solution)/shard_map/ppermute | solution.py:32
  549.8 14.8 %collective-permute-done.43 = bf16[256,1536]{1,0:T(8,128)(2,1)S(1)} collective-permute-done((bf16[256,1536]{1,0:T(8,128)(2,1)}, bf16[256,1536]{1,0:T(8,128)(2,1)S(1)}, u32[]{:S(2)}, u32[]{:S(2)}) %collective-permute-start.43) | collective-permute-done | bytes 786464 | tf_op jit(solution)/shard_map/ppermute | solution.py:32
  564.7 2.0 maximum_select_fusion
  574.0 44.1 %all-gather.5.cloned.1.call-done = bf16[256,5120]{1,0:T(8,128)(2,1)} async-done(((bf16[32,5120]{1,0:T(8,128)(2,1)}), bf16[256,5120]{1,0:T(8,128)(2,1)}) %all-gather.5.cloned.1.call-update) | async-done | bytes 2621456 | tf_op jit(solution)/shard_map/all_gather | solution.py:982
  619.2 2.2 fusion
  (396 shorter events, 182.1 us)
Async XLA Ops:
  7.2 559.5 %all-gather.3.cloned.1.call-start = ((), (), s32[]{:S(2)}) async-start(), calls=%async_computation | async-start | bytes 1179648 | tf_op jit(solution)/shard_map/all_gather | solution.py:982
  13.1 16.3 %collective-permute-start.1 = (bf16[576,512]{1,0:T(8,128)(2,1)S(1)}, bf16[576,512]{1,0:T(8,128)(2,1)S(1)}, u32[]{:S(2)}, u32[]{:S(2)}) collective-permute-start(bf16[576,512]{1,0:T(8,128)(2,1)S(1)} %pack_0.1), channel_id=1, source_target_pairs={{0,2},{1,3},{2,0},{3,1},{4,6},{5,7},{6,4},{7,5},{8,10},{9,11},{10,... | collective-permute-start | bytes 1769480 | tf_op jit(solution)/shard_map/ppermute | solution.py:32
  32.2 9.0 %collective-permute-start.2 = (bf16[288,512]{1,0:T(8,128)(2,1)}, bf16[288,512]{1,0:T(8,128)(2,1)S(1)}, u32[]{:S(2)}, u32[]{:S(2)}) collective-permute-start(bf16[288,512]{1,0:T(8,128)(2,1)} %get-tuple-element.96), channel_id=1, source_target_pairs={{0,2},{1,3},{2,0},{3,1},{4,6},{5,7},{6,4},{7,5},{8,10},{9,11},{10,... | collective-permute-start | bytes 884744 | tf_op jit(solution)/shard_map/ppermute | solution.py:32
  33.9 7.9 %collective-permute-start.3 = (bf16[288,512]{1,0:T(8,128)(2,1)}, bf16[288,512]{1,0:T(8,128)(2,1)}, u32[]{:S(2)}, u32[]{:S(2)}) collective-permute-start(bf16[288,512]{1,0:T(8,128)(2,1)} %get-tuple-element.97), channel_id=1, source_target_pairs={{0,8},{1,9},{2,10},{3,11},{4,12},{5,13},{6,14},{7,15},{8,0},{9,1},... | collective-permute-start | bytes 884744 | tf_op jit(solution)/shard_map/ppermute | solution.py:32
  35.5 7.6 %collective-permute-start.4 = (bf16[288,512]{1,0:T(8,128)(2,1)}, bf16[288,512]{1,0:T(8,128)(2,1)}, u32[]{:S(2)}, u32[]{:S(2)}) collective-permute-start(bf16[288,512]{1,0:T(8,128)(2,1)} %get-tuple-element.98), channel_id=1, source_target_pairs={{0,4},{1,5},{2,6},{3,7},{4,0},{5,1},{6,2},{7,3},{8,12},{9,13},{10,... | collective-permute-start | bytes 884744 | tf_op jit(solution)/shard_map/ppermute | solution.py:32
  37.0 107.9 %collective-permute-start.26 = (bf16[384,1536]{1,0:T(8,128)(2,1)}, bf16[384,1536]{1,0:T(8,128)(2,1)}, u32[]{:S(2)}, u32[]{:S(2)}) collective-permute-start(bf16[384,1536]{1,0:T(8,128)(2,1)} %refs_0_.27), channel_id=1, source_target_pairs={{0,1},{1,0},{2,3},{3,2},{4,5},{5,4},{6,7},{7,6},{8,9},{9,8},{10,11... | collective-permute-start | bytes 3538952 | tf_op jit(solution)/shard_map/ppermute | solution.py:32
  47.8 28.7 %collective-permute-start.6 = (bf16[720,512]{1,0:T(8,128)(2,1)}, bf16[720,512]{1,0:T(8,128)(2,1)}, u32[]{:S(2)}, u32[]{:S(2)}) collective-permute-start(bf16[720,512]{1,0:T(8,128)(2,1)} %get-tuple-element.100), channel_id=1, source_target_pairs={{0,8},{1,9},{2,10},{3,11},{4,12},{5,13},{6,14},{7,15},{8,0},{9,1},... | collective-permute-start | bytes 2211848 | tf_op jit(solution)/shard_map/ppermute | solution.py:32
  48.3 28.2 %collective-permute-start.7 = (bf16[720,512]{1,0:T(8,128)(2,1)}, bf16[720,512]{1,0:T(8,128)(2,1)}, u32[]{:S(2)}, u32[]{:S(2)}) collective-permute-start(bf16[720,512]{1,0:T(8,128)(2,1)} %get-tuple-element.101), channel_id=1, source_target_pairs={{0,4},{1,5},{2,6},{3,7},{4,0},{5,1},{6,2},{7,3},{8,12},{9,13},{10,... | collective-permute-start | bytes 2211848 | tf_op jit(solution)/shard_map/ppermute | solution.py:32
  50.8 25.7 %collective-permute-start.5 = (bf16[576,512]{1,0:T(8,128)(2,1)}, bf16[576,512]{1,0:T(8,128)(2,1)}, u32[]{:S(2)}, u32[]{:S(2)}) collective-permute-start(bf16[576,512]{1,0:T(8,128)(2,1)} %get-tuple-element.99), channel_id=1, source_target_pairs={{0,2},{1,3},{2,0},{3,1},{4,6},{5,7},{6,4},{7,5},{8,10},{9,11},{10,... | collective-permute-start | bytes 1769480 | tf_op jit(solution)/shard_map/ppermute | solution.py:32
  75.0 38.6 %collective-permute-start.32 = (bf16[16,6912]{1,0:T(8,128)(2,1)}, bf16[16,6912]{1,0:T(8,128)(2,1)}, u32[]{:S(2)}, u32[]{:S(2)}) collective-permute-start(bf16[16,6912]{1,0:T(8,128)(2,1)} %concatenate.67), channel_id=1, source_target_pairs={{0,2},{1,3},{2,0},{3,1},{4,6},{5,7},{6,4},{7,5},{8,10},{9,11},{10,... | collective-permute-start | bytes 663560 | tf_op jit(solution)/shard_map/ppermute | solution.py:32
  82.9 19.2 %collective-permute-start.10 = (bf16[576,512]{1,0:T(8,128)(2,1)}, bf16[576,512]{1,0:T(8,128)(2,1)}, u32[]{:S(2)}, u32[]{:S(2)}) collective-permute-start(bf16[576,512]{1,0:T(8,128)(2,1)} %get-tuple-element.104), channel_id=1, source_target_pairs={{0,4},{1,5},{2,6},{3,7},{4,0},{5,1},{6,2},{7,3},{8,12},{9,13},{10,... | collective-permute-start | bytes 1769480 | tf_op jit(solution)/shard_map/ppermute | solution.py:32
  83.4 18.6 %collective-permute-start.8 = (bf16[576,512]{1,0:T(8,128)(2,1)}, bf16[576,512]{1,0:T(8,128)(2,1)}, u32[]{:S(2)}, u32[]{:S(2)}) collective-permute-start(bf16[576,512]{1,0:T(8,128)(2,1)} %get-tuple-element.102), channel_id=1, source_target_pairs={{0,2},{1,3},{2,0},{3,1},{4,6},{5,7},{6,4},{7,5},{8,10},{9,11},{10,... | collective-permute-start | bytes 1769480 | tf_op jit(solution)/shard_map/ppermute | solution.py:32
  84.0 18.0 %collective-permute-start.9 = (bf16[576,512]{1,0:T(8,128)(2,1)}, bf16[576,512]{1,0:T(8,128)(2,1)}, u32[]{:S(2)}, u32[]{:S(2)}) collective-permute-start(bf16[576,512]{1,0:T(8,128)(2,1)} %get-tuple-element.103), channel_id=1, source_target_pairs={{0,8},{1,9},{2,10},{3,11},{4,12},{5,13},{6,14},{7,15},{8,0},{9,1},... | collective-permute-start | bytes 1769480 | tf_op jit(solution)/shard_map/ppermute | solution.py:32
  102.1 11.6 %collective-permute-start.31 = (bf16[16,6912]{1,0:T(8,128)(2,1)}, bf16[16,6912]{1,0:T(8,128)(2,1)}, u32[]{:S(2)}, u32[]{:S(2)}) collective-permute-start(bf16[16,6912]{1,0:T(8,128)(2,1)} %concatenate.66), channel_id=1, source_target_pairs={{0,1},{1,0},{2,3},{3,2},{4,5},{5,4},{6,7},{7,6},{8,9},{9,8},{10,11... | collective-permute-start | bytes 663560 | tf_op jit(solution)/shard_map/ppermute | solution.py:32
  108.9 22.4 %collective-permute-start.16 = (bf16[864,512]{1,0:T(8,128)(2,1)}, bf16[864,512]{1,0:T(8,128)(2,1)}, u32[]{:S(2)}, u32[]{:S(2)}) collective-permute-start(bf16[864,512]{1,0:T(8,128)(2,1)} %get-tuple-element.107), channel_id=1, source_target_pairs={{0,8},{1,9},{2,10},{3,11},{4,12},{5,13},{6,14},{7,15},{8,0},{9,1},... | collective-permute-start | bytes 2654216 | tf_op jit(solution)/shard_map/ppermute | solution.py:32
  110.5 15.8 %collective-permute-start.15 = (bf16[576,512]{1,0:T(8,128)(2,1)}, bf16[576,512]{1,0:T(8,128)(2,1)}, u32[]{:S(2)}, u32[]{:S(2)}) collective-permute-start(bf16[576,512]{1,0:T(8,128)(2,1)} %get-tuple-element.106), channel_id=1, source_target_pairs={{0,2},{1,3},{2,0},{3,1},{4,6},{5,7},{6,4},{7,5},{8,10},{9,11},{10,... | collective-permute-start | bytes 1769480 | tf_op jit(solution)/shard_map/ppermute | solution.py:32
  113.6 22.5 %collective-permute-start.17 = (bf16[864,512]{1,0:T(8,128)(2,1)}, bf16[864,512]{1,0:T(8,128)(2,1)}, u32[]{:S(2)}, u32[]{:S(2)}) collective-permute-start(bf16[864,512]{1,0:T(8,128)(2,1)} %copy-done.36), channel_id=1, source_target_pairs={{0,4},{1,5},{2,6},{3,7},{4,0},{5,1},{6,2},{7,3},{8,12},{9,13},{10,... | collective-permute-start | bytes 2654216 | tf_op jit(solution)/shard_map/ppermute | solution.py:32
  115.3 28.1 %collective-permute-start.27 = (bf16[384,768]{1,0:T(8,128)(2,1)}, bf16[384,768]{1,0:T(8,128)(2,1)}, u32[]{:S(2)}, u32[]{:S(2)}) collective-permute-start(bf16[384,768]{1,0:T(8,128)(2,1)} %refs_1_.21), channel_id=1, source_target_pairs={{0,1},{1,0},{2,3},{3,2},{4,5},{5,4},{6,7},{7,6},{8,9},{9,8},{10,11... | collective-permute-start | bytes 1769480 | tf_op jit(solution)/shard_map/ppermute | solution.py:32
  126.3 17.2 %collective-permute-start.28 = (bf16[384,768]{1,0:T(8,128)(2,1)}, bf16[384,768]{1,0:T(8,128)(2,1)}, u32[]{:S(2)}, u32[]{:S(2)}) collective-permute-start(bf16[384,768]{1,0:T(8,128)(2,1)} %refs_2_.23), channel_id=1, source_target_pairs={{0,1},{1,0},{2,3},{3,2},{4,5},{5,4},{6,7},{7,6},{8,9},{9,8},{10,11... | collective-permute-start | bytes 1769480 | tf_op jit(solution)/shard_map/ppermute | solution.py:32
  131.3 66.8 %collective-permute-start.12 = (bf16[384,4096]{1,0:T(8,128)(2,1)S(1)}, bf16[384,4096]{1,0:T(8,128)(2,1)}, u32[]{:S(2)}, u32[]{:S(2)}) collective-permute-start(bf16[384,4096]{1,0:T(8,128)(2,1)S(1)} %copy-done), channel_id=1, source_target_pairs={{0,1},{1,0},{2,3},{3,2},{4,5},{5,4},{6,7},{7,6},{8,9},{9,8},{10,11... | collective-permute-start | bytes 9437192 | tf_op jit(solution)/shard_map/ppermute | solution.py:32
  136.2 10.4 %collective-permute-start = (bf16[384,1536]{1,0:T(8,128)(2,1)}, bf16[384,1536]{1,0:T(8,128)(2,1)S(1)}, u32[]{:S(2)}, u32[]{:S(2)}) collective-permute-start(bf16[384,1536]{1,0:T(8,128)(2,1)} %refs_0_.26), channel_id=1, source_target_pairs={{0,1},{1,0},{2,3},{3,2},{4,5},{5,4},{6,7},{7,6},{8,9},{9,8},{10,11... | collective-permute-start | bytes 3538952 | tf_op jit(solution)/shard_map/ppermute | solution.py:32
  143.4 56.1 %collective-permute-start.29 = (bf16[2304,512]{1,0:T(8,128)(2,1)}, bf16[2304,512]{1,0:T(8,128)(2,1)}, u32[]{:S(2)}, u32[]{:S(2)}) collective-permute-start(bf16[2304,512]{1,0:T(8,128)(2,1)} %get-tuple-element.116.refs_6_), channel_id=1, source_target_pairs={{0,1},{1,0},{2,3},{3,2},{4,5},{5,4},{6,7},{7,6},{8,9},{9,8},{10,11... | collective-permute-start | bytes 7077896 | tf_op jit(solution)/shard_map/ppermute | solution.py:32
  143.5 22.4 %collective-permute-start.19 = (bf16[864,512]{1,0:T(8,128)(2,1)}, bf16[864,512]{1,0:T(8,128)(2,1)}, u32[]{:S(2)}, u32[]{:S(2)}) collective-permute-start(bf16[864,512]{1,0:T(8,128)(2,1)} %get-tuple-element.110), channel_id=1, source_target_pairs={{0,8},{1,9},{2,10},{3,11},{4,12},{5,13},{6,14},{7,15},{8,0},{9,1},... | collective-permute-start | bytes 2654216 | tf_op jit(solution)/shard_map/ppermute | solution.py:32
  144.9 21.7 %collective-permute-start.20 = (bf16[864,512]{1,0:T(8,128)(2,1)}, bf16[864,512]{1,0:T(8,128)(2,1)}, u32[]{:S(2)}, u32[]{:S(2)}) collective-permute-start(bf16[864,512]{1,0:T(8,128)(2,1)} %get-tuple-element.111), channel_id=1, source_target_pairs={{0,4},{1,5},{2,6},{3,7},{4,0},{5,1},{6,2},{7,3},{8,12},{9,13},{10,... | collective-permute-start | bytes 2654216 | tf_op jit(solution)/shard_map/ppermute | solution.py:32
  146.6 15.1 %collective-permute-start.18 = (bf16[576,512]{1,0:T(8,128)(2,1)}, bf16[576,512]{1,0:T(8,128)(2,1)}, u32[]{:S(2)}, u32[]{:S(2)}) collective-permute-start(bf16[576,512]{1,0:T(8,128)(2,1)} %get-tuple-element.109), channel_id=1, source_target_pairs={{0,2},{1,3},{2,0},{3,1},{4,6},{5,7},{6,4},{7,5},{8,10},{9,11},{10,... | collective-permute-start | bytes 1769480 | tf_op jit(solution)/shard_map/ppermute | solution.py:32
  161.7 20.0 %collective-permute-start.30 = (bf16[256,1536]{1,0:T(8,128)(2,1)}, bf16[256,1536]{1,0:T(8,128)(2,1)S(1)}, u32[]{:S(2)}, u32[]{:S(2)}) collective-permute-start(bf16[256,1536]{1,0:T(8,128)(2,1)} %copy-done.37), channel_id=1, source_target_pairs={{0,3},{1,2},{2,1},{3,0},{4,7},{5,6},{6,5},{7,4},{8,11},{9,10},{10,... | collective-permute-start | bytes 2359304 | tf_op jit(solution)/shard_map/ppermute | solution.py:32
  165.8 53.1 %collective-permute-start.11 = (bf16[1152,512]{1,0:T(8,128)(2,1)}, bf16[1152,512]{1,0:T(8,128)(2,1)}, u32[]{:S(2)}, u32[]{:S(2)}) collective-permute-start(bf16[1152,512]{1,0:T(8,128)(2,1)} %copy-done.20), channel_id=1, source_target_pairs={{0,1},{1,0},{2,3},{3,2},{4,5},{5,4},{6,7},{7,6},{8,9},{9,8},{10,11... | collective-permute-start | bytes 3538952 | tf_op jit(solution)/shard_map/ppermute | solution.py:32
  166.6 31.5 %collective-permute-start.36 = (bf16[256,1536]{1,0:T(8,128)(2,1)}, bf16[256,1536]{1,0:T(8,128)(2,1)S(1)}, u32[]{:S(2)}, u32[]{:S(2)}) collective-permute-start(bf16[256,1536]{1,0:T(8,128)(2,1)} %copy-done.38), channel_id=1, source_target_pairs={{0,3},{1,2},{2,1},{3,0},{4,7},{5,6},{6,5},{7,4},{8,11},{9,10},{10,... | collective-permute-start | bytes 2359304 | tf_op jit(solution)/shard_map/ppermute | solution.py:32
  181.7 132.5 %collective-permute-start.13 = (bf16[384,4096]{1,0:T(8,128)(2,1)}, bf16[384,4096]{1,0:T(8,128)(2,1)}, u32[]{:S(2)}, u32[]{:S(2)}) collective-permute-start(bf16[384,4096]{1,0:T(8,128)(2,1)} %refs_1_.20), channel_id=1, source_target_pairs={{0,1},{1,0},{2,3},{3,2},{4,5},{5,4},{6,7},{7,6},{8,9},{9,8},{10,11... | collective-permute-start | bytes 9437192 | tf_op jit(solution)/shard_map/ppermute | solution.py:32
  198.1 116.7 %collective-permute-start.14 = (bf16[1024,1536]{1,0:T(8,128)(2,1)}, bf16[1024,1536]{1,0:T(8,128)(2,1)}, u32[]{:S(2)}, u32[]{:S(2)}) collective-permute-start(bf16[1024,1536]{1,0:T(8,128)(2,1)} %refs_2_.22), channel_id=1, source_target_pairs={{0,1},{1,0},{2,3},{3,2},{4,5},{5,4},{6,7},{7,6},{8,9},{9,8},{10,11... | collective-permute-start | bytes 9437192 | tf_op jit(solution)/shard_map/ppermute | solution.py:32
  199.0 22.8 %collective-permute-start.21 = (bf16[864,512]{1,0:T(8,128)(2,1)}, bf16[864,512]{1,0:T(8,128)(2,1)S(1)}, u32[]{:S(2)}, u32[]{:S(2)}) collective-permute-start(bf16[864,512]{1,0:T(8,128)(2,1)} %get-tuple-element.112), channel_id=1, source_target_pairs={{0,4},{1,5},{2,6},{3,7},{4,0},{5,1},{6,2},{7,3},{8,12},{9,13},{10,... | collective-permute-start | bytes 2654216 | tf_op jit(solution)/shard_map/ppermute | solution.py:32
  199.5 22.8 %collective-permute-start.22 = (bf16[864,512]{1,0:T(8,128)(2,1)}, bf16[864,512]{1,0:T(8,128)(2,1)}, u32[]{:S(2)}, u32[]{:S(2)}) collective-permute-start(bf16[864,512]{1,0:T(8,128)(2,1)} %get-tuple-element.113), channel_id=1, source_target_pairs={{0,8},{1,9},{2,10},{3,11},{4,12},{5,13},{6,14},{7,15},{8,0},{9,1},... | collective-permute-start | bytes 2654216 | tf_op jit(solution)/shard_map/ppermute | solution.py:32
  218.9 10.0 %collective-permute-start.34 = (bf16[8,512,96]{1,2,0:T(8,128)(2,1)}, bf16[8,512,96]{1,2,0:T(8,128)(2,1)}, u32[]{:S(2)}, u32[]{:S(2)}) collective-permute-start(bf16[8,512,96]{1,2,0:T(8,128)(2,1)} %copy.167), channel_id=1, source_target_pairs={{0,1},{1,0},{2,3},{3,2},{4,5},{5,4},{6,7},{7,6},{8,9},{9,8},{10,11... | collective-permute-start | bytes 2359304 | tf_op jit(solution)/shard_map/ppermute | solution.py:32
  221.8 93.0 %collective-permute-start.39 = (bf16[2304,512]{1,0:T(8,128)(2,1)}, bf16[2304,512]{1,0:T(8,128)(2,1)}, u32[]{:S(2)}, u32[]{:S(2)}) collective-permute-start(bf16[2304,512]{1,0:T(8,128)(2,1)} %copy-done.32), channel_id=1, source_target_pairs={{0,1},{1,0},{2,3},{3,2},{4,5},{5,4},{6,7},{7,6},{8,9},{9,8},{10,11... | collective-permute-start | bytes 7077896 | tf_op jit(solution)/shard_map/ppermute | solution.py:32
  222.3 10.6 %collective-permute-start.35 = (bf16[8,512,96]{1,2,0:T(8,128)(2,1)}, bf16[8,512,96]{1,2,0:T(8,128)(2,1)}, u32[]{:S(2)}, u32[]{:S(2)}) collective-permute-start(bf16[8,512,96]{1,2,0:T(8,128)(2,1)} %copy.168), channel_id=1, source_target_pairs={{0,1},{1,0},{2,3},{3,2},{4,5},{5,4},{6,7},{7,6},{8,9},{9,8},{10,11... | collective-permute-start | bytes 2359304 | tf_op jit(solution)/shard_map/ppermute | solution.py:32
  228.9 15.7 %collective-permute-start.23 = (bf16[576,512]{1,0:T(8,128)(2,1)S(1)}, bf16[576,512]{1,0:T(8,128)(2,1)S(1)}, u32[]{:S(2)}, u32[]{:S(2)}) collective-permute-start(bf16[576,512]{1,0:T(8,128)(2,1)S(1)} %get-tuple-element.114), channel_id=1, source_target_pairs={{0,8},{1,9},{2,10},{3,11},{4,12},{5,13},{6,14},{7,15},{8,0},{9,1},... | collective-permute-start | bytes 1769480 | tf_op jit(solution)/shard_map/ppermute | solution.py:32
  233.0 107.6 %collective-permute-start.38 = (bf16[2304,512]{1,0:T(8,128)(2,1)}, bf16[2304,512]{1,0:T(8,128)(2,1)}, u32[]{:S(2)}, u32[]{:S(2)}) collective-permute-start(bf16[2304,512]{1,0:T(8,128)(2,1)} %copy-done.33), channel_id=1, source_target_pairs={{0,1},{1,0},{2,3},{3,2},{4,5},{5,4},{6,7},{7,6},{8,9},{9,8},{10,11... | collective-permute-start | bytes 7077896 | tf_op jit(solution)/shard_map/ppermute | solution.py:32
  244.6 14.9 %collective-permute-start.24 = (bf16[576,512]{1,0:T(8,128)(2,1)S(1)}, bf16[576,512]{1,0:T(8,128)(2,1)S(1)}, u32[]{:S(2)}, u32[]{:S(2)}) collective-permute-start(bf16[576,512]{1,0:T(8,128)(2,1)S(1)} %get-tuple-element.115), channel_id=1, source_target_pairs={{0,4},{1,5},{2,6},{3,7},{4,0},{5,1},{6,2},{7,3},{8,12},{9,13},{10,... | collective-permute-start | bytes 1769480 | tf_op jit(solution)/shard_map/ppermute | solution.py:32
  260.3 109.2 %collective-permute-start.37 = (bf16[2304,512]{1,0:T(8,128)(2,1)}, bf16[2304,512]{1,0:T(8,128)(2,1)}, u32[]{:S(2)}, u32[]{:S(2)}) collective-permute-start(bf16[2304,512]{1,0:T(8,128)(2,1)} %copy-done.34), channel_id=1, source_target_pairs={{0,1},{1,0},{2,3},{3,2},{4,5},{5,4},{6,7},{7,6},{8,9},{9,8},{10,11... | collective-permute-start | bytes 7077896 | tf_op jit(solution)/shard_map/ppermute | solution.py:32
  314.2 83.9 %collective-permute-start.25 = (bf16[2304,512]{1,0:T(8,128)(2,1)}, bf16[2304,512]{1,0:T(8,128)(2,1)}, u32[]{:S(2)}, u32[]{:S(2)}) collective-permute-start(bf16[2304,512]{1,0:T(8,128)(2,1)} %pack_8.1.refs_6_), channel_id=1, source_target_pairs={{0,1},{1,0},{2,3},{3,2},{4,5},{5,4},{6,7},{7,6},{8,9},{9,8},{10,11... | collective-permute-start | bytes 7077896 | tf_op jit(solution)/shard_map/ppermute | solution.py:32
  479.2 5.7 collective-permute-start.41
  480.6 6.6 %collective-permute-start.42 = (bf16[8,512,96]{1,2,0:T(8,128)(2,1)}, bf16[8,512,96]{1,2,0:T(8,128)(2,1)}, u32[]{:S(2)}, u32[]{:S(2)}) collective-permute-start(bf16[8,512,96]{1,2,0:T(8,128)(2,1)} %copy.185), channel_id=1, source_target_pairs={{0,1},{1,0},{2,3},{3,2},{4,5},{5,4},{6,7},{7,6},{8,9},{9,8},{10,11... | collective-permute-start | bytes 2359304 | tf_op jit(solution)/shard_map/ppermute | solution.py:32
  515.5 6.6 %collective-permute-start.46 = (bf16[2,16,4992]{2,1,0:T(8,128)(2,1)S(1)}, bf16[2,16,4992]{2,1,0:T(8,128)(2,1)S(1)}, u32[]{:S(2)}, u32[]{:S(2)}) collective-permute-start(bf16[2,16,4992]{2,1,0:T(8,128)(2,1)S(1)} %select_convert_fusion), channel_id=1, source_target_pairs={{0,1},{1,0},{2,3},{3,2},{4,5},{5,4},{6,7},{7,6},{8,9},{9,8},{10,11... | collective-permute-start | bytes 958472 | tf_op jit(solution)/shard_map/ppermute | solution.py:32
  516.8 4.3 collective-permute-start.45
  521.9 96.2 %all-gather.5.cloned.1.call-start = ((), (), s32[]{:S(2)}) async-start(), calls=%async_computation.1 | async-start | bytes 2949120 | tf_op jit(solution)/shard_map/all_gather | solution.py:982
  522.3 5.3 collective-permute-start.47
  528.5 19.9 %collective-permute-start.40 = (bf16[256,1536]{1,0:T(8,128)(2,1)S(1)}, bf16[256,1536]{1,0:T(8,128)(2,1)S(1)}, u32[]{:S(2)}, u32[]{:S(2)}) collective-permute-start(bf16[256,1536]{1,0:T(8,128)(2,1)S(1)} %get-tuple-element.231), channel_id=1, source_target_pairs={{0,3},{1,2},{2,1},{3,0},{4,7},{5,6},{6,5},{7,4},{8,11},{9,10},{10,... | collective-permute-start | bytes 2359304 | tf_op jit(solution)/shard_map/ppermute | solution.py:32
  528.6 35.9 %collective-permute-start.43 = (bf16[256,1536]{1,0:T(8,128)(2,1)}, bf16[256,1536]{1,0:T(8,128)(2,1)S(1)}, u32[]{:S(2)}, u32[]{:S(2)}) collective-permute-start(bf16[256,1536]{1,0:T(8,128)(2,1)} %get-tuple-element.155), channel_id=1, source_target_pairs={{0,3},{1,2},{2,1},{3,0},{4,7},{5,6},{6,5},{7,4},{8,11},{9,10},{10,... | collective-permute-start | bytes 2359304 | tf_op jit(solution)/shard_map/ppermute | solution.py:32
  (66 other events, 631.2 us)
Sparse Core Ops, SparseCore 0:
  522.0 39.8 all-gather.2
  564.7 53.3 all-gather.4
